TPU v7x, 256 devices: a whole 4x4x8 slice. The times are simulated.
256 devices in a mesh: expert: 32 (over x, y, core), seq: 8 (over z).
Axes of the slice: x: 4, y: 4, z: 8, core: 2. Of those that a mesh axis runs over, the one named last changes fastest.
Arguments:
- resid: bfloat16 [65536, 2048], P(('expert', 'seq')), may hold values from -6 to 6
- gate_in: bfloat16 [65536, 2048], P(('expert', 'seq')), may hold values from -6 to 6
- gate_short: float32 [3, 2048], replicated, may hold values from -3 to 3
- value_short: float32 [3, 2048], replicated, may hold values from -3 to 3
- long_filter: bfloat16 [4096, 2048], P('expert', 'seq'), may hold values from -2 to 2
- skip_gain: float32 [2048], P('seq'), may hold values from -3 to 3
- norm_gain: float32 [2048], replicated, may hold values from 0.5 to 1.5
- expert_ids: int32 [65536, 4], P(('expert', 'seq')), may hold values from 0 to 63, all different within a row; in each aligned block of 256 rows (0 to 255, 256 to 511, ...) at most 24 rows name the same one
- gate_wts: float32 [65536, 4], P(('expert', 'seq')), may hold values from 0.05 to 0.6
- spare_pick: int32 [32], replicated, may hold values from 0 to 1
- w_gate: bfloat16 [64, 2048, 256], P('expert'), may hold values from -0.125 to 0.125
- w_up: bfloat16 [64, 2048, 256], P('expert'), may hold values from -0.125 to 0.125
- w_down: bfloat16 [64, 2048, 256], P('expert'), may hold values from -0.375 to 0.375
Outputs:
- mixed: bfloat16 [65536, 2048], P(('expert', 'seq'))
Inputs may be any that keep to these rules, and one draw needn't show every extreme that they name: `expert_ids`: in each aligned block of 256 tokens no expert is named by more than 24 entries, and some expert by exactly that many; each token names 4 different experts.
All inputs are finite; a program needn't handle non-finite values.
Results may differ from a plain program's by a relative error of at most 0.0051.
Values may be sent and summed in bfloat16 or wider, within the bound.
A program may use at most 128 MiB of HBM per device.

v0:
```python
import math

import jax
import jax.numpy as jnp
from jax import lax
from jax.sharding import PartitionSpec as P

precise = lax.Precision.HIGH


def passed_along(block, axis, distance):
    devices = range(lax.axis_size(axis))
    route = [(i - distance, i) for i in devices if i - distance in devices]
    return lax.ppermute(block, axis, route)


def from_partner(array, axis, apart):
    return lax.ppermute(array, axis, [(i, i ^ 1 << apart) for i in range(lax.axis_size(axis))])


def angle_table(count_rows, count_cols, period):
    row_ids = jnp.arange(count_rows, dtype=jnp.int32)[:, None]
    col_ids = jnp.arange(count_cols, dtype=jnp.int32)[None, :]
    angle = 2.0 * math.pi / period * (row_ids * col_ids % period).astype(jnp.float32)
    return (jnp.cos(angle), jnp.sin(angle))


def local_conv(signal, kernel, rim):
    widened = signal.astype(jnp.float32)
    extended = jnp.concatenate([rim.astype(jnp.float32), widened], axis=0)
    return kernel[0] * widened + kernel[1] * extended[1:-1] + kernel[2] * extended[:-2]


def alternating(signal, inner):
    chans = signal.shape[1]
    shaped = signal.astype(jnp.float32).reshape(signal.shape[0] // inner, inner, chans)
    signs = (1 - 2 * (jnp.arange(inner, dtype=jnp.int32) % 2)).astype(jnp.float32)
    return jnp.sum(shaped * signs[None, :, None], axis=(0, 1))


def forward_spectrum(signal, outer, inner):
    chans = signal.shape[1]
    cos_b, sin_b = angle_table(outer, outer // 2, outer)
    first_table = jnp.concatenate([cos_b, -sin_b], axis=0)
    flat = signal.astype(jnp.float32).reshape(outer // 2, inner * chans)
    section = jnp.dot(first_table, flat, precision=precise).reshape(2, outer, inner, chans)
    cos_w, sin_w = angle_table(outer, inner, outer * inner)
    cos_w = cos_w[:, :, None]
    sin_w = sin_w[:, :, None]
    real_z = section[0] * cos_w + section[1] * sin_w
    imag_z = section[1] * cos_w - section[0] * sin_w
    turned = jnp.stack([real_z, imag_z]).transpose(0, 2, 1, 3).reshape(2 * inner, outer * chans)
    cos_a, sin_a = angle_table(inner // 2, inner, inner)
    second_table = jnp.concatenate(
        [jnp.concatenate([cos_a, sin_a], axis=1), jnp.concatenate([-sin_a, cos_a], axis=1)], axis=0
    )
    return jnp.dot(second_table, turned, precision=precise).reshape(2, inner // 2, outer, chans)


def inverse_spectrum(product, outer, inner):
    chans = product.shape[3]
    cos_a, sin_a = angle_table(inner, inner // 2, inner)
    first_table = jnp.concatenate(
        [jnp.concatenate([cos_a, -sin_a], axis=1), jnp.concatenate([sin_a, cos_a], axis=1)], axis=0
    )
    section = jnp.dot(
        first_table, product.reshape(inner, outer * chans), precision=precise
    ).reshape(2, inner, outer, chans)
    cos_w, sin_w = angle_table(inner, outer, outer * inner)
    cos_w = cos_w[:, :, None]
    sin_w = sin_w[:, :, None]
    real_v = section[0] * cos_w - section[1] * sin_w
    imag_v = section[1] * cos_w + section[0] * sin_w
    turned = jnp.stack([real_v, imag_v]).transpose(0, 2, 1, 3).reshape(2 * outer, inner * chans)
    cos_b, sin_b = angle_table(outer // 2, outer, outer)
    last_table = jnp.concatenate([cos_b, -sin_b], axis=1)
    return jnp.dot(last_table, turned, precision=precise).reshape(outer // 2 * inner, chans)


def long_convolution(sequence, filt, skip, outer):
    seq_len, chans = sequence.shape
    inner = 2 * seq_len // outer
    spec_h = forward_spectrum(filt, outer, inner)
    spec_v = forward_spectrum(sequence, outer, inner)
    real_p = spec_h[0] * spec_v[0] - spec_h[1] * spec_v[1]
    imag_p = spec_h[0] * spec_v[1] + spec_h[1] * spec_v[0]
    first_bin = (jnp.arange(inner // 2, dtype=jnp.int32)[:, None] == 0) & (
        jnp.arange(outer, dtype=jnp.int32)[None, :] == 0
    )
    halving = jnp.where(first_bin, 0.5, 1.0).astype(jnp.float32)[:, :, None]
    product = jnp.stack([real_p * halving, imag_p * halving])
    period = float(2 * seq_len)
    conv = inverse_spectrum(product, outer, inner) * (2.0 / period)
    nyquist = alternating(filt, inner) * alternating(sequence, inner) / period
    signs = (1 - 2 * (jnp.arange(inner, dtype=jnp.int32) % 2)).astype(jnp.float32)
    conv = (
        conv.reshape(seq_len // inner, inner, chans) + signs[None, :, None] * nyquist[None, None, :]
    ).reshape(seq_len, chans)
    return (conv + skip * sequence.astype(jnp.float32)).astype(jnp.bfloat16)


def expert_ffn(rows, gate_w, up_w, down_w):
    gate = jnp.dot(rows, gate_w, preferred_element_type=jnp.float32)
    upper = jnp.dot(rows, up_w, preferred_element_type=jnp.float32)
    act = (jax.nn.silu(gate) * upper).astype(jnp.bfloat16)
    return lax.dot_general(
        act, down_w, (((1,), (1,)), ((), ())), preferred_element_type=jnp.float32
    ).astype(jnp.bfloat16)


def body(
    resid,
    gate_in,
    gate_short,
    value_short,
    long_filter,
    skip_gain,
    norm_gain,
    expert_ids,
    gate_wts,
    spare_pick,
    w_gate,
    w_up,
    w_down,
):
    n_seq = lax.axis_size("seq")
    n_exp = lax.axis_size("expert")
    me = lax.axis_index("expert")
    row_index = lax.axis_index("seq")
    len_dev, width = resid.shape
    exp_dev = w_gate.shape[0]
    topk = expert_ids.shape[1]
    parity = me % 2
    chans = width // (2 * n_seq)
    half_len = len_dev * n_seq
    filter_whole = lax.all_gather(long_filter, "expert", axis=0, tiled=True)
    filter_mine = lax.dynamic_slice_in_dim(filter_whole, parity * chans, chans, 1)
    skip_mine = lax.dynamic_slice_in_dim(skip_gain, parity * chans, chans, 0)
    tails = jnp.stack([gate_in[-2:], resid[-2:]])
    rims = passed_along(tails, ("expert", "seq"), 1)
    at_start = (row_index == 0) & (parity == 0)
    rims = jnp.where(at_start, jnp.zeros((), jnp.bfloat16), rims)
    gated = local_conv(gate_in, gate_short, rims[0])
    values = local_conv(resid, value_short, rims[1]).astype(jnp.bfloat16)
    columns = lax.all_to_all(values, "seq", split_axis=1, concat_axis=0, tiled=True)
    keeping = lax.dynamic_slice_in_dim(columns, parity * chans, chans, 1)
    leaving = lax.dynamic_slice_in_dim(columns, (1 - parity) * chans, chans, 1)
    partner_half = from_partner(leaving, "expert", 0)
    first_half = jnp.where(parity == 0, keeping, partner_half)
    second_half = jnp.where(parity == 0, partner_half, keeping)
    sequence = jnp.concatenate([first_half, second_half], axis=0)
    longconv = long_convolution(sequence, filter_mine, skip_mine, len_dev)
    own_rows = lax.dynamic_slice_in_dim(longconv, parity * half_len, half_len, 0)
    other_rows = lax.dynamic_slice_in_dim(longconv, (1 - parity) * half_len, half_len, 0)
    came_back = from_partner(other_rows, "expert", 0)
    lower = jnp.where(parity == 0, own_rows, came_back)
    upper_part = jnp.where(parity == 0, came_back, own_rows)
    block = jnp.concatenate([lower, upper_part], axis=1)
    back = lax.all_to_all(block, "seq", split_axis=0, concat_axis=1, tiled=True)
    hidden = resid.astype(jnp.float32) + gated * back.astype(jnp.float32)
    scale = lax.rsqrt(jnp.mean(hidden * hidden, axis=-1, keepdims=True) + 1e-05)
    normed = (hidden * scale * norm_gain).astype(jnp.bfloat16)
    experts_all = exp_dev * n_exp
    cap = 3 * len_dev * topk // (4 * experts_all)
    entries = len_dev * topk
    ids = expert_ids.reshape(entries)
    wts = gate_wts.reshape(entries)
    onehot = (ids[:, None] == jnp.arange(experts_all, dtype=jnp.int32)[None, :]).astype(jnp.int32)
    rank = jnp.sum((jnp.cumsum(onehot, axis=0) - onehot) * onehot, axis=1)
    home = ids // exp_dev
    local = ids % exp_dev
    partner = (home + n_exp // 2) % n_exp
    picked = jnp.sum(
        jnp.where(
            partner[:, None] == jnp.arange(n_exp, dtype=jnp.int32)[None, :], spare_pick[None, :], 0
        ),
        axis=1,
    )
    replicated = picked == local
    kept = (rank < cap) | (rank < 2 * cap) & replicated
    depth = 2 * cap
    total = n_exp * exp_dev * depth
    flat = jnp.where(kept, (home * exp_dev + local) * depth + rank, total)
    row_tok = (
        jnp.zeros((total,), jnp.int32)
        .at[flat]
        .set(jnp.arange(entries, dtype=jnp.int32) // topk, mode="drop")
    )
    row_live = jnp.zeros((total,), jnp.int32).at[flat].set(1, mode="drop")
    send = jnp.where(row_live[:, None] > 0, normed[row_tok], jnp.zeros((), jnp.bfloat16))
    received = lax.all_to_all(
        send.reshape(n_exp, exp_dev, depth, width),
        "expert",
        split_axis=0,
        concat_axis=0,
        tiled=True,
    )
    results = []
    for index in range(exp_dev):
        rows = received[:, index].reshape(n_exp * depth, width)
        results.append(
            expert_ffn(rows, w_gate[index], w_up[index], w_down[index]).reshape(n_exp, depth, width)
        )
    outputs = jnp.stack(results, axis=1)
    returned = lax.all_to_all(outputs, "expert", split_axis=0, concat_axis=0, tiled=True).reshape(
        total, width
    )
    lookup = jnp.where(kept, flat, 0).reshape(len_dev, topk)
    weight = jnp.where(kept, wts, 0.0).reshape(len_dev, topk)
    moe = jnp.zeros((len_dev, width), jnp.float32)
    for choice_index in range(topk):
        moe = moe + weight[:, choice_index : choice_index + 1] * returned[
            lookup[:, choice_index]
        ].astype(jnp.float32)
    return (hidden + moe).astype(jnp.bfloat16)


def solution(mesh):
    placed = (
        P(("expert", "seq"), None),
        P(("expert", "seq"), None),
        P(),
        P(),
        P("expert", "seq"),
        P("seq"),
        P(),
        P(("expert", "seq"), None),
        P(("expert", "seq"), None),
        P(),
        P("expert", None, None),
        P("expert", None, None),
        P("expert", None, None),
    )
    return jax.shard_map(
        body, mesh=mesh, in_specs=placed, out_specs=P(("expert", "seq"), None), check_vma=False
    )
```

profile of v0, /device:TPU:40, one launch (start us, length us, event | category | flops | bytes accessed | tf_op | source)
XLA Modules:
  0.0 452.6 jit_solution(13931142574303873218)
XLA Ops:
  7.4 3.8 collective-permute-start
  15.9 9.2 %all-to-all-start = ((bf16[256,8,256]{2,0,1:T(8,128)(2,1)}), bf16[256,8,256]{2,0,1:T(8,128)(2,1)S(1)}, u32[]{:S(2)}, u32[]{:S(2)}) async-start(bf16[256,8,256]{2,0,1:T(8,128)(2,1)} %bitcast.151), calls=%async_computation | async-start | bytes 2097152 | tf_op jit(solution)/shard_map/all_to_all | solution.py:145
  31.1 20.2 %all-to-all-done = bf16[256,8,256]{2,0,1:T(8,128)(2,1)S(1)} async-done(((bf16[256,8,256]{2,0,1:T(8,128)(2,1)}), bf16[256,8,256]{2,0,1:T(8,128)(2,1)S(1)}, u32[]{:S(2)}, u32[]{:S(2)}) %all-to-all-start) | async-done | bytes 1048608 | tf_op jit(solution)/shard_map/all_to_all | solution.py:145
  58.8 2.7 copy.154
  61.5 2.7 copy.155
  64.2 13.9 %all-gather.2.cloned.1.call-done = bf16[4096,256]{1,0:T(8,128)(2,1)} async-done(((bf16[128,256]{1,0:T(8,128)(2,1)}), bf16[4096,256]{1,0:T(8,128)(2,1)}) %all-gather.2.cloned.1.call-update) | async-done | bytes 2097168 | tf_op jit(solution)/shard_map/all_gather | solution.py:136
  78.1 5.3 %fusion.26 = (f32[128]{0:T(128)}, f32[128]{0:T(128)}, bf16[4096,128]{1,0:T(8,128)(2,1)S(1)}) fusion(f32[4096]{0:T(1024)S(1)} %copy-done.15, bf16[2048,128]{1,0:T(8,128)(2,1)S(1)} %get-tuple-element.39, bf16[2048,128]{1,0:T(8,128)(2,1)S(1)} %get-tuple-element.38, bf16[4096,256]{1,0:T(8,128)(2,1)} %all-gather.2.cloned.1.call-done, s32[]{:T(128)S(6)} %select_n.286), kind=kLoop, calls=%fused_computation.57 | loop fusion | flops 4718336 | bytes 3163140 | tf_op jit(solution)/shard_map/reduce_sum | solution.py:38
  91.5 19.0 %multiply_add_fusion.2 = (f32[1,256,32,128]{3,1,2,0:T(8,128)S(1)}, f32[1,256,32,128]{3,1,2,0:T(8,128)S(1)}, f32[1,256,32,128]{3,1,2,0:T(8,128)S(1)}, f32[1,256,32,128]{3,1,2,0:T(8,128)}) fusion(f32[1,256,32,128]{3,2,1,0:T(8,128)S(1)} %bitcast.163, f32[1,256,32,128]{3,2,1,0:T(8,128)S(1)} %bitcast.162, f32[256,32]{0,1:T(8,128)S(1)} %copy-done.11, ...), kind=kLoop, calls=%fused_computation.37 | loop fusion | flops 12582912 | bytes 33619968 | tf_op jit(solution)/shard_map/add | solution.py:50
  111.5 3.0 pad_maximum_fusion.1
  114.5 7.4 %fusion.6 = f32[32,32768]{1,0:T(8,128)S(1)} fusion(f32[8,8,256,128]{3,2,1,0:T(8,128)S(1)} %bitcast.154, f32[16,32]{1,0:T(8,128)S(1)} %copy-done.13, f32[16,32]{1,0:T(8,128)S(1)} %fusion.149, f32[16,32]{1,0:T(8,128)S(1)} %get-tuple-element.58), kind=kOutput, calls=%fused_computation.13 | convolution fusion | flops 402659328 | bytes 12589056 | tf_op jit(solution)/shard_map/dot_general | solution.py:57
  122.0 7.6 %fusion.3 = f32[32,32768]{1,0:T(8,128)S(1)} fusion(f32[8,8,256,128]{3,2,1,0:T(8,128)S(1)} %bitcast.153, f32[16,32]{1,0:T(8,128)S(1)} %copy-done.13, f32[16,32]{1,0:T(8,128)S(1)} %fusion.149, f32[16,32]{1,0:T(8,128)S(1)} %get-tuple-element.58), kind=kOutput, calls=%fused_computation.10 | convolution fusion | flops 402659328 | bytes 12589056 | tf_op jit(solution)/shard_map/dot_general | solution.py:57
  132.7 5.9 %fusion.12 = f32[64,32768]{1,0:T(8,128)S(1)} fusion(f32[4,8,256,128]{3,2,1,0:T(8,128)S(1)} %bitcast.157, f32[32,16]{1,0:T(8,128)S(1)} %copy-done.18, f32[32,16]{1,0:T(8,128)S(1)} %copy-done.17, f32[32,16]{1,0:T(8,128)S(1)} %copy-done.16), kind=kOutput, calls=%fused_computation.22 | convolution fusion | flops 402659328 | bytes 12589056 | tf_op jit(solution)/shard_map/dot_general | solution.py:66
  140.8 9.5 %multiply_subtract_fusion = (f32[1,32,256,128]{3,1,2,0:T(8,128)S(1)}, f32[1,32,256,128]{3,1,2,0:T(8,128)S(1)}) fusion(f32[1,32,256,128]{3,2,1,0:T(8,128)S(1)} %bitcast.159, f32[1,32,256,128]{3,2,1,0:T(8,128)S(1)} %bitcast.158, f32[32,256]{0,1:T(8,128)S(1)} %copy-done.9, f32[32,256]{0,1:T(8,128)S(1)} %copy-done.10), kind=kLoop, calls=%fused_computation.33 | loop fusion | flops 6291456 | bytes 16842752 | tf_op jit(solution)/shard_map/sub | solution.py:72
  151.4 8.2 %fusion.9 = f32[128,4096]{1,0:T(8,128)} fusion(f32[64,8,32,128]{3,2,1,0:T(8,128)S(1)} %bitcast.155, f32[128,256]{1,0:T(8,128)S(1)} %get-tuple-element.64, f32[128,256]{1,0:T(8,128)S(1)} %copy-done.8), kind=kOutput, calls=%fused_computation.21 | convolution fusion | flops 1611202560 | bytes 10747904 | tf_op jit(solution)/shard_map/dot_general | solution.py:77
  167.2 7.6 %all-to-all-start.1 = ((bf16[8,256,256]{2,1,0:T(8,128)(2,1)}), bf16[8,256,256]{2,1,0:T(8,128)(2,1)S(1)}, u32[]{:S(2)}, u32[]{:S(2)}) async-start(bf16[8,256,256]{2,1,0:T(8,128)(2,1)} %bitcast.17), calls=%async_computation.1 | async-start | bytes 2097152 | tf_op jit(solution)/shard_map/all_to_all | solution.py:159
  176.5 18.0 %reduce-window.6 = s32[64,8,128]{2,1,0:T(8,128)S(1)} reduce-window(s32[64,8,128]{2,1,0:T(8,128)S(1)} %fusion.69, s32[]{:T(128)} %constant.182.clone.1), window={size=1x1x128 pad=0_0x0_0x127_0}, to_apply=%region_2.3 | reduce-window | flops 8323072 | bytes 524292 | tf_op jit(solution)/shard_map/reduce-window
  195.3 4.3 scatter_custom_fusion.1
  199.6 4.5 scatter_custom_fusion
  207.8 7.0 %gather_fusion = bf16[1536,2048]{1,0:T(8,128)(2,1)} fusion(bf16[256,2048]{1,0:T(8,128)(2,1)S(1)} %multiply_convert_fusion, s32[2048]{0:T(1024)S(1)} %pad_clamp_fusion), kind=kCustom, calls=%fused_computation | custom fusion | bytes 12589056 | tf_op jit(solution)/shard_map/gather | solution.py:190
  214.8 3.3 broadcast_select_fusion
  218.1 77.4 %all_to_all.42 = bf16[32,2,24,2048]{3,2,1,0:T(8,128)(2,1)S(1)} all-to-all(bf16[32,2,24,2048]{3,2,1,0:T(8,128)(2,1)S(1)} %broadcast_select_fusion), channel_id=1, replica_groups=mesh['expert'=32,'seq'=8] {'expert'}, dimensions={0} | all-to-all | bytes 12582912 | tf_op jit(solution)/shard_map/all_to_all | solution.py:191
  297.1 2.5 fusion.41
  300.6 7.7 %convolution_convert_fusion.1 = bf16[768,2048]{1,0:T(8,128)(2,1)} fusion(bf16[768,2048]{1,0:T(8,128)(2,1)} %bitcast.173, bf16[2,2048,256]{2,1,0:T(8,128)(2,1)} %param.25, bf16[2,2048,256]{2,1,0:T(8,128)(2,1)} %param.24, f32[768,256]{1,0:T(8,128)} %fusion.41), kind=kOutput, calls=%fused_computation.39 | convolution fusion | flops 1613365248 | bytes 9175040 | tf_op jit(solution)/shard_map/dot_general | solution.py:106
  308.3 7.4 %convolution_convert_fusion = bf16[768,2048]{1,0:T(8,128)(2,1)} fusion(bf16[768,2048]{1,0:T(8,128)(2,1)} %bitcast.171, bf16[2,2048,256]{2,1,0:T(8,128)(2,1)} %param.25, bf16[2,2048,256]{2,1,0:T(8,128)(2,1)} %param.24, f32[768,256]{1,0:T(8,128)S(1)} %fusion.36), kind=kOutput, calls=%fused_computation.38 | convolution fusion | flops 1613365248 | bytes 9175040 | tf_op jit(solution)/shard_map/dot_general | solution.py:106
  315.7 6.0 %pad_maximum_fusion.3 = bf16[32,2,24,2048]{3,2,1,0:T(8,128)(2,1)} fusion(bf16[32,1,24,2048]{3,2,1,0:T(8,128)(2,1)} %bitcast.175, bf16[32,1,24,2048]{3,2,1,0:T(8,128)(2,1)} %bitcast.174), kind=kLoop, calls=%fused_computation.19 | loop fusion | flops 3145728 | bytes 12582912 | tf_op jit(solution)/shard_map/stack | solution.py:204
  321.8 6.3 %all-to-all-start.3 = ((bf16[32,2,24,2048]{3,2,1,0:T(8,128)(2,1)}), bf16[32,2,24,2048]{3,2,1,0:T(8,128)(2,1)}, u32[]{:S(2)}, u32[]{:S(2)}) async-start(bf16[32,2,24,2048]{3,2,1,0:T(8,128)(2,1)} %pad_maximum_fusion.3), calls=%async_computation.3 | async-start | bytes 12582912 | tf_op jit(solution)/shard_map/all_to_all | solution.py:205
  329.7 85.3 %all-to-all-done.3 = bf16[32,2,24,2048]{3,2,1,0:T(8,128)(2,1)} async-done(((bf16[32,2,24,2048]{3,2,1,0:T(8,128)(2,1)}), bf16[32,2,24,2048]{3,2,1,0:T(8,128)(2,1)}, u32[]{:S(2)}, u32[]{:S(2)}) %all-to-all-start.3) | async-done | bytes 6291488 | tf_op jit(solution)/shard_map/all_to_all | solution.py:205
  414.9 6.0 %gather_fusion.1 = bf16[256,2048]{1,0:T(8,128)(2,1)S(1)} fusion(bf16[1536,2048]{1,0:T(8,128)(2,1)} %bitcast.37, s32[1024]{0:T(1024)S(1)} %get-tuple-element.69), kind=kCustom, calls=%fused_computation.1 | custom fusion | bytes 2098176 | tf_op jit(solution)/shard_map/gather | solution.py:212
  420.9 7.0 %gather_fusion.2 = bf16[256,2048]{1,0:T(8,128)(2,1)} fusion(bf16[1536,2048]{1,0:T(8,128)(2,1)} %bitcast.37, s32[1024]{0:T(1024)S(1)} %get-tuple-element.68), kind=kCustom, calls=%fused_computation.2 | custom fusion | bytes 2098176 | tf_op jit(solution)/shard_map/gather | solution.py:212
  427.9 6.9 %gather_fusion.3 = bf16[256,2048]{1,0:T(8,128)(2,1)} fusion(bf16[1536,2048]{1,0:T(8,128)(2,1)} %bitcast.37, s32[1024]{0:T(1024)S(1)} %get-tuple-element.67), kind=kCustom, calls=%fused_computation.3 | custom fusion | bytes 2098176 | tf_op jit(solution)/shard_map/gather | solution.py:212
  434.8 6.9 %gather_fusion.4 = bf16[256,2048]{1,0:T(8,128)(2,1)} fusion(bf16[1536,2048]{1,0:T(8,128)(2,1)} %bitcast.37, s32[1024]{0:T(1024)S(1)} %get-tuple-element.66), kind=kCustom, calls=%fused_computation.4 | custom fusion | bytes 2098176 | tf_op jit(solution)/shard_map/gather | solution.py:212
  441.8 3.8 add_convert_fusion
  (164 shorter events, 51.7 us)
Async XLA Ops:
  7.4 6.2 %collective-permute-start = (bf16[2,2,2048]{2,1,0:T(2,128)(2,1)S(1)}, bf16[2,2,2048]{2,1,0:T(2,128)(2,1)S(1)}, u32[]{:S(2)}, u32[]{:S(2)}) collective-permute-start(bf16[2,2,2048]{2,1,0:T(2,128)(2,1)S(1)} %pad_maximum_fusion.12), channel_id=1, source_target_pairs={{0,1},{1,2},{2,3},{3,4},{4,5},{5,6},{6,7},{7,8},{8,9},{9,10},{10,1... | collective-permute-start | bytes 49160 | tf_op jit(solution)/shard_map/ppermute | solution.py:14
  14.2 12.8 %copy-start.31 = (f32[256]{0:T(256)S(1)}, f32[256]{0:T(256)}, u32[]{:S(2)}) copy-start(f32[256]{0:T(256)} %param.18) | copy-start | bytes 3076
  15.9 35.3 %all-to-all-start = ((bf16[256,8,256]{2,0,1:T(8,128)(2,1)}), bf16[256,8,256]{2,0,1:T(8,128)(2,1)S(1)}, u32[]{:S(2)}, u32[]{:S(2)}) async-start(bf16[256,8,256]{2,0,1:T(8,128)(2,1)} %bitcast.151), calls=%async_computation | async-start | bytes 2097152 | tf_op jit(solution)/shard_map/all_to_all | solution.py:145
  25.1 53.0 %all-gather.2.cloned.1.call-start = ((), (), s32[]{:S(2)}) async-start(), calls=%async_computation.4 | async-start | bytes 2162688 | tf_op jit(solution)/shard_map/all_gather | solution.py:136
  51.3 3.2 collective-permute-start.1
  61.5 16.6 %copy-start.15 = (f32[4096]{0:T(1024)S(1)}, f32[4096]{0:T(1024)}, u32[]{:S(2)}) copy-start(f32[4096]{0:T(1024)} %mul.892) | copy-start | bytes 49156
  87.2 1.6 copy-start.11
  87.2 1.6 copy-start.12
  88.0 2.2 copy-start
  88.0 3.5 copy-start.1
  111.5 3.0 copy-start.13
  150.4 1.0 copy-start.8
  159.6 1.8 copy-start.27
  159.6 1.8 copy-start.28
  159.6 1.8 copy-start.25
  159.6 1.9 copy-start.26
  161.4 1.8 copy-start.21
  161.8 1.0 copy-start.4
  162.9 2.0 collective-permute-start.2
  163.6 11.2 %copy-start.7 = (bf16[256,2048]{1,0:T(8,128)(2,1)S(1)}, bf16[256,2048]{1,0:T(8,128)(2,1)}, u32[]{:S(2)}) copy-start(bf16[256,2048]{1,0:T(8,128)(2,1)} %param.14) | copy-start | bytes 3145732
  167.2 27.8 %copy-start.29 = (s32[32]{0:T(128)S(1)}, s32[32]{0:T(128)}, u32[]{:S(2)}) copy-start(s32[32]{0:T(128)} %param.22) | copy-start | bytes 388
  167.2 37.2 %all-to-all-start.1 = ((bf16[8,256,256]{2,1,0:T(8,128)(2,1)}), bf16[8,256,256]{2,1,0:T(8,128)(2,1)S(1)}, u32[]{:S(2)}, u32[]{:S(2)}) async-start(bf16[8,256,256]{2,1,0:T(8,128)(2,1)} %bitcast.17), calls=%async_computation.1 | async-start | bytes 2097152 | tf_op jit(solution)/shard_map/all_to_all | solution.py:159
  174.8 29.5 %copy-start.20 = (f32[3,2048]{1,0:T(4,128)S(1)}, f32[3,2048]{1,0:T(4,128)}, u32[]{:S(2)}) copy-start(f32[3,2048]{1,0:T(4,128)} %param.15) | copy-start | bytes 73732
  204.3 1.2 copy-start.3
  204.3 1.2 copy-start.14
  204.4 1.9 copy-start.2
  206.3 1.3 copy-start.22
  295.5 1.6 copy-start.30
  296.6 3.0 copy-start.6
  296.6 3.0 copy-start.5
  321.8 6.8 %copy-start.23 = (f32[256,4]{0,1:T(4,128)S(1)}, f32[256,4]{0,1:T(4,128)}, u32[]{:S(2)}) copy-start(f32[256,4]{0,1:T(4,128)} %param.21) | copy-start | bytes 12292
  321.8 93.2 %all-to-all-start.3 = ((bf16[32,2,24,2048]{3,2,1,0:T(8,128)(2,1)}), bf16[32,2,24,2048]{3,2,1,0:T(8,128)(2,1)}, u32[]{:S(2)}, u32[]{:S(2)}) async-start(bf16[32,2,24,2048]{3,2,1,0:T(8,128)(2,1)} %pad_maximum_fusion.3), calls=%async_computation.3 | async-start | bytes 12582912 | tf_op jit(solution)/shard_map/all_to_all | solution.py:205
  (7 other events, 5.3 us)
Sparse Core Ops, SparseCore 0:
  28.5 49.5 all-gather.1
where the time goes:
time: 457 us; the launch traced here: 453 us
  waiting for transfers between devices  121 us (26%)
  other arithmetic  88.2 us (19%)
  blocking collectives  77.4 us (17%)
  local copies, waits for them, and re-layouts  71.5 us (16%)
  matrix products  52.4 us (11%)
  starting transfers between devices  27.4 us (6%)
  between operations  14.5 us (3%)
    all_to_all x1, waiting for transfers between devices, body(): lax.all_to_all(outputs, 'expert', split_axis=0, concat_axis=0, tiled=True)  85.3 us
    all_to_all x1, blocking collectives, body(): lax.all_to_all(send.reshape(n_exp, exp_dev, depth, width), 'expert', spli...  77.4 us
    gather x4, local copies, waits for them, and re-layouts, body(): returned[lookup[:, choice_index]].astype(jnp.float32)  26.8 us
    all_to_all x1, waiting for transfers between devices, body(): lax.all_to_all(values, 'seq', split_axis=1, concat_axis=0, tiled=True)  20.2 us
    add x1, other arithmetic, forward_spectrum(): real_z = section[0] * cos_w + section[1] * sin_w  19 us
    unnamed x77, local copies, waits for them, and re-layouts  18.9 us
    another operation x3, other arithmetic  18.2 us
    dot_general x2, matrix products, expert_ffn(): lax.dot_general(act, down_w, (((1,), (1,)), ((), ())), preferred_element_...  15.1 us
  transfers between devices with their start and end apart: 7, of which 4 were waited for; matrix products, arithmetic and copies ran while one was open for 11% of the time, Pallas kernels for 0%

commit v1 on v0

v1 whole, which is shorter than its diff:
```python
import functools

import jax
import jax.numpy as jnp
from jax import lax
from jax.experimental import pallas as pl
from jax.experimental.pallas import tpu as pltpu
from jax.sharding import PartitionSpec as P

F32, BF16, I32 = jnp.float32, jnp.bfloat16, jnp.int32
VMEM_LIMIT = 56 * 1024 * 1024
TOK = 256
WIDTH = 2048
HOMES = 32
GROUPS = 8
SEQS = 16
BLOCKS = 16
CH = 8
POS = SEQS * TOK
QUARTERS = 4
QW = WIDTH // QUARTERS
MAIN = 32
LEFT = 4
MSG = QUARTERS * (MAIN + LEFT)
CAP = 12
HID = 256
PAD = 128


def iota(shape, dim):
    return lax.broadcasted_iota(I32, shape, dim)


def eye(n):
    return (iota((n, n), 0) == iota((n, n), 1)).astype(BF16)


def nt(a, b):
    return lax.dot_general(a, b, (((1,), (1,)), ((), ())), preferred_element_type=F32)


def mm(a, b):
    return jnp.dot(a, b, preferred_element_type=F32)


def short_conv(x, before2, before1, kernel):
    row = iota(x.shape, 0)
    back1 = jnp.where(row == 0, before1, pltpu.roll(x, 1, 0))
    back2 = jnp.where(row == 0, before2, jnp.where(row == 1, before1, pltpu.roll(x, 2, 0)))
    return kernel[0:1] * x + kernel[1:2] * back1 + kernel[2:3] * back2


def group_cols(g):
    return pl.ds(pl.multiple_of(g * 256, 256), 256)


def to_message(block):
    first = block[:, :128].reshape(32, 8, 128)
    second = block[:, 128:].reshape(32, 8, 128)
    return jnp.concatenate([first, second], axis=1).astype(BF16)


def from_message(message):
    wide = message.astype(F32)
    first = wide[:, :8].reshape(256, 128).astype(BF16)
    second = wide[:, 8:].reshape(256, 128).astype(BF16)
    ident = eye(128)
    return jnp.concatenate([nt(ident, first), nt(ident, second)], axis=0)


def values_kernel(resid_ref, rim_ref, kern_ref, filt_ref, out_ref, filt_out_ref):
    ident = eye(256)

    def one(g, _):
        cols = group_cols(g)
        x = resid_ref[:, cols].astype(F32)
        values = short_conv(x, rim_ref[2:3, cols], rim_ref[3:4, cols], kern_ref[:, cols]).astype(BF16)
        out_ref[:, g] = to_message(nt(ident, values))
        return 0

    lax.fori_loop(0, GROUPS, one, 0)
    filt_out_ref[...] = nt(ident, filt_ref[...]).reshape(HOMES, CH, 128)


def build_bank(row, bank_ref):
    wide = jnp.concatenate([jnp.broadcast_to(row, (8, POS)), jnp.zeros((8, PAD), F32)], axis=1)
    base = pltpu.roll(wide, 0, 1, stride=1, stride_axis=0)
    for a in range(8):
        upper = pltpu.roll(base, 16 * a, 1) if a else base
        lower = pltpu.roll(base, 16 * a + 8, 1)
        both = jnp.concatenate([upper, lower], axis=0)[:, :POS].astype(BF16)
        bank_ref[16 * a : 16 * a + 16, :] = both
        bank_ref[128 + 16 * a : 144 + 16 * a, PAD:] = both[:, : POS - PAD]


def conv_kernel(recv_ref, filt_ref, skip_ref, out_ref, wide_ref, hrow_ref, x_ref, y_ref, bank_ref, acc_ref):
    for e in range(HOMES):
        hrow_ref[:, 128 * e : 128 * e + 128] = filt_ref[e]
    bank_ref[128:, :PAD] = jnp.zeros((128, PAD), BF16)
    for i in range(BLOCKS):
        wide_ref[i * 256 : i * 256 + 256] = recv_ref[:, i].astype(F32).reshape(256, 128)
    for c in range(CH):
        for half in range(2):
            x_ref[c, :, 128 * half : 128 * half + 128] = wide_ref[pl.ds(8 * half + c, 256, stride=16), :]

    def one(c, _):
        build_bank(hrow_ref[pl.ds(c, 1), :], bank_ref)
        x = x_ref[c]
        lhs = x.astype(BF16)
        acc_ref[...] = x * skip_ref[pl.ds(c, 1), :]
        for k in range(BLOCKS):
            acc_ref[16 * k :, :] += mm(lhs[: 256 - 16 * k], bank_ref[:, 256 * k : 256 * k + 256])
        y_ref[c] = acc_ref[...]
        return 0

    lax.fori_loop(0, CH, one, 0)
    for c in range(CH):
        for half in range(2):
            wide_ref[pl.ds(8 * half + c, 256, stride=16), :] = y_ref[c, :, 128 * half : 128 * half + 128]
    for i in range(BLOCKS):
        out_ref[:, i] = wide_ref[i * 256 : i * 256 + 256].reshape(SEQS, 16, 128).astype(BF16)


def slots(named, rep, axis):
    tri = (iota((TOK, TOK), axis) < iota((TOK, TOK), 1 - axis)).astype(BF16)
    if axis == 0:
        rank = mm(named.astype(BF16), tri)
    else:
        rank = mm(tri, named.astype(BF16))
    kept = (named > 0) & ((rank < CAP) | ((rank < 2 * CAP) & (rep > 0)))
    return jnp.where(kept, jnp.where(rep > 0, rank, rank + 2 * CAP), -1.0)


def norm_kernel(
    back_ref, resid_ref, gate_in_ref, rim_ref, kern_ref, gain_ref, idst_ref, rep_ref, send_ref, hid_ref, normed_ref, slot_ref
):
    hid_ref, send_ref = hid_ref, send_ref

    def one(g, total):
        cols = group_cols(g)
        x = gate_in_ref[:, cols].astype(F32)
        gated = short_conv(x, rim_ref[0:1, cols], rim_ref[1:2, cols], kern_ref[:, cols])
        hidden = resid_ref[:, cols].astype(F32) + gated * from_message(back_ref[:, g])
        hid_ref[:, cols] = hidden
        return total + jnp.sum(hidden * hidden, axis=1, keepdims=True)

    total = lax.fori_loop(0, GROUPS, one, jnp.zeros((TOK, 1), F32))
    scale = lax.rsqrt(total * (1.0 / WIDTH) + 1e-05)

    def two(g, _):
        cols = group_cols(g)
        normed_ref[:, cols] = (hid_ref[:, cols] * scale * gain_ref[:, cols]).astype(BF16)
        return 0

    lax.fori_loop(0, GROUPS, two, 0)
    named = jnp.zeros((64, TOK), F32)
    for k in range(4):
        named += (idst_ref[k : k + 1, :] == iota((64, TOK), 0)).astype(F32)
    slot_ref[...] = slots(named, rep_ref[...], 0)

    def four(h, _):
        rows = MAIN * 8
        sel = []
        left = []
        for j in range(8):
            even = slot_ref[pl.ds(16 * h + 2 * j, 1), :]
            odd = slot_ref[pl.ds(16 * h + 2 * j + 1, 1), :]
            r = iota((MAIN, TOK), 0).astype(F32)
            sel.append(((even == r) | (odd == r)).astype(BF16))
            r = (iota((16, TOK), 0) % 4 + MAIN).astype(F32)
            left.append(((even == r) | (odd == r)).astype(F32))
        sel = jnp.concatenate(sel, axis=0)
        left = jnp.concatenate(left, axis=0)
        part = iota((128, TOK), 0) % 16 // 4
        spill = jnp.zeros((128, QW), F32)
        for q in range(QUARTERS):
            cols = normed_ref[:, QW * q : QW * q + QW]
            send_ref[pl.ds(8 * h, 8), MAIN * q : MAIN * q + MAIN, :] = mm(sel, cols).astype(BF16).reshape(8, MAIN, QW)
            spill += mm(jnp.where(part == q, left, 0.0).astype(BF16), cols)
        send_ref[pl.ds(8 * h, 8), MAIN * QUARTERS :, :] = spill.astype(BF16).reshape(8, 16, QW)
        return 0

    lax.fori_loop(0, HOMES // 8, four, 0)


def silu_mul(gate, up):
    return gate / (1.0 + jnp.exp(-gate)) * up


def ffn_group(first, n, recv_ref, wg_ref, wu_ref, wd_ref, out_ref, hot):
    cold = 1 - hot
    src = pl.ds(first, n)
    rows = 16 * n
    zero = functools.partial(jnp.zeros, (rows, HID), F32)
    ga, ua, gb, ub, gc, uc, gl, ul = (zero() for _ in range(8))
    left = recv_ref[src, MAIN * QUARTERS :, :].reshape(rows, QW)
    part = iota((rows, HID), 0) % 16 // 4
    for q in range(QUARTERS):
        xa = recv_ref[src, MAIN * q : MAIN * q + 16, :].reshape(rows, QW)
        xb = recv_ref[src, MAIN * q + 16 : MAIN * q + 32, :].reshape(rows, QW)
        cut = slice(QW * q, QW * q + QW)
        both = jnp.concatenate([xa, xb], axis=0)
        gh, uh = mm(both, wg_ref[hot, cut, :]), mm(both, wu_ref[hot, cut, :])
        ga, ua, gb, ub = ga + gh[:rows], ua + uh[:rows], gb + gh[rows:], ub + uh[rows:]
        both = jnp.concatenate([xb, left], axis=0)
        gh, uh = mm(both, wg_ref[cold, cut, :]), mm(both, wu_ref[cold, cut, :])
        gc, uc = gc + gh[:rows], uc + uh[:rows]
        gl = gl + jnp.where(part == q, gh[rows:], 0.0)
        ul = ul + jnp.where(part == q, uh[rows:], 0.0)

    def over_quarters(acc):
        acc = acc.reshape(n, 16, HID)
        acc = acc[:, :8] + acc[:, 8:]
        acc = acc.reshape(8 * n, HID)
        low = iota(acc.shape, 0) % 8 < 4
        other = jnp.where(low, pltpu.roll(acc, 8 * n - 4, 0), pltpu.roll(acc, 4, 0))
        acc = (acc + other).reshape(n, 8, HID)
        return jnp.concatenate([acc, acc], axis=1).reshape(rows, HID)

    is_hot = iota((rows, HID), 0) % 16 < 8
    act_a = silu_mul(ga, ua).astype(BF16)
    act_b = silu_mul(jnp.where(is_hot, gb, gc), jnp.where(is_hot, ub, uc))
    act_bh = jnp.where(is_hot, act_b, 0.0).astype(BF16)
    act_bc = jnp.where(is_hot, 0.0, act_b).astype(BF16)
    act_l = silu_mul(over_quarters(gl), over_quarters(ul)).astype(BF16)
    hot_in = jnp.concatenate([act_a, act_bh], axis=0)
    cold_in = jnp.concatenate([act_bc, act_l], axis=0)
    part = iota((rows, QW), 0) % 16 // 4
    spill = jnp.zeros((rows, QW), F32)
    for q in range(QUARTERS):
        cut = slice(QW * q, QW * q + QW)
        oh = nt(hot_in, wd_ref[hot, cut, :])
        oc = nt(cold_in, wd_ref[cold, cut, :])
        out_ref[src, MAIN * q : MAIN * q + 16, :] = oh[:rows].astype(BF16).reshape(n, 16, QW)
        out_ref[src, MAIN * q + 16 : MAIN * q + 32, :] = (oh[rows:] + oc[:rows]).astype(BF16).reshape(n, 16, QW)
        spill = jnp.where(part == q, oc[rows:], spill)
    out_ref[src, MAIN * QUARTERS :, :] = spill.astype(BF16).reshape(n, 16, QW)


def ffn_kernel(hot_ref, recv_ref, wg_ref, wu_ref, wd_ref, out_ref):
    hot = hot_ref[0]

    def one(i, _):
        ffn_group(16 * i, 16, recv_ref, wg_ref, wu_ref, wd_ref, out_ref, hot)
        return 0

    lax.fori_loop(0, HOMES // 16, one, 0)


def combine_weights(ids_ref, wts_ref, rep_ref, wmain_ref, wleft_ref):
    named = jnp.zeros((TOK, 64), F32)
    weight = jnp.zeros((TOK, 64), F32)
    for k in range(4):
        hit = ids_ref[:, k : k + 1] == iota((TOK, 64), 1)
        named += hit.astype(F32)
        weight += jnp.where(hit, wts_ref[:, k : k + 1], 0.0)
    slot = slots(named, rep_ref[...], 1).astype(BF16)
    whi = weight.astype(BF16)
    wlo = (weight - whi.astype(F32)).astype(BF16)

    def spread(per, want, block):
        lanes = HOMES * per // 4
        lane = iota((64, lanes), 1) + block * lanes
        expert = iota((64, lanes), 0)
        high = low = jnp.zeros((TOK, lanes), F32)
        for odd in range(2):
            pick = (expert == 2 * (lane // per) + odd).astype(BF16)
            hit = mm(slot, pick) == want
            high = high + jnp.where(hit, mm(whi, pick), 0.0)
            low = low + jnp.where(hit, mm(wlo, pick), 0.0)
        return high.astype(BF16), low.astype(BF16)

    for block in range(4):
        want = (iota((TOK, 8 * MAIN), 1) % MAIN).astype(F32)
        high, low = spread(MAIN, want, block)
        wmain_ref[0, :, 256 * block : 256 * block + 256] = high
        wmain_ref[1, :, 256 * block : 256 * block + 256] = low
        want = (iota((TOK, 8 * 16), 1) % 4 + MAIN).astype(F32)
        high, low = spread(16, want, block)
        wleft_ref[0, :, 128 * block : 128 * block + 128] = high
        wleft_ref[1, :, 128 * block : 128 * block + 128] = low


def combine_kernel(ret_ref, hid_ref, ids_ref, wts_ref, rep_ref, out_ref, wmain_ref, wleft_ref):
    combine_weights(ids_ref, wts_ref, rep_ref, wmain_ref, wleft_ref)
    left = ret_ref[:, MAIN * QUARTERS :, :].reshape(HOMES * 16, QW)
    part = iota((TOK, HOMES * 16), 1) % 16 // 4
    for q in range(QUARTERS):
        main = ret_ref[:, MAIN * q : MAIN * q + MAIN, :].reshape(HOMES * MAIN, QW)
        moe = mm(wmain_ref[0], main) + mm(wmain_ref[1], main)
        for w in range(2):
            moe += mm(jnp.where(part == q, wleft_ref[w].astype(F32), 0.0).astype(BF16), left)
        cut = slice(QW * q, QW * q + QW)
        out_ref[:, cut] = (hid_ref[:, cut] + moe).astype(BF16)


def whole(n):
    return [pl.BlockSpec(memory_space=pltpu.VMEM)] * n


def call(kernel, outs, scratch, *args, smem=0):
    return pl.pallas_call(
        kernel,
        out_shape=outs,
        in_specs=[pl.BlockSpec(memory_space=pltpu.SMEM)] * smem + whole(len(args) - smem),
        out_specs=whole(1)[0] if not isinstance(outs, tuple) else tuple(whole(len(outs))),
        scratch_shapes=scratch,
        compiler_params=pltpu.CompilerParams(vmem_limit_bytes=VMEM_LIMIT),
    )(*args)


def body(
    resid,
    gate_in,
    gate_short,
    value_short,
    long_filter,
    skip_gain,
    norm_gain,
    expert_ids,
    gate_wts,
    spare_pick,
    w_gate,
    w_up,
    w_down,
):
    n_seq = lax.axis_size("seq")
    n_exp = lax.axis_size("expert")
    me = lax.axis_index("expert")
    z = lax.axis_index("seq")
    tails = jnp.stack([gate_in[-2:], resid[-2:]])
    count = n_exp * n_seq
    rims = lax.ppermute(tails, ("expert", "seq"), [(i, i + 1) for i in range(count - 1)])
    rims = jnp.where((z == 0) & (me % 2 == 0), jnp.zeros((), BF16), rims)
    rims = rims.astype(F32).reshape(4, WIDTH)
    sds = jax.ShapeDtypeStruct
    values, filt = call(
        values_kernel,
        (sds((HOMES, GROUPS, 16, 128), BF16), sds((HOMES, CH, 128), F32)),
        [],
        resid,
        rims,
        value_short,
        long_filter,
    )
    both = ("expert", "seq")
    values = lax.all_to_all(values.reshape(256, 16, 128), both, split_axis=0, concat_axis=0, tiled=True)
    filt = lax.all_to_all(filt, "expert", split_axis=0, concat_axis=0, tiled=True)
    skip = lax.dynamic_slice_in_dim(skip_gain, me * CH, CH, 0)
    skip = jnp.broadcast_to(skip[:, None], (CH, 256))
    conv = call(
        conv_kernel,
        sds((SEQS, BLOCKS, 16, 128), BF16),
        [
            pltpu.VMEM((POS, 128), F32),
            pltpu.VMEM((CH, POS), F32),
            pltpu.VMEM((CH, 256, 256), F32),
            pltpu.VMEM((CH, 256, 256), F32),
            pltpu.VMEM((256, POS), BF16),
            pltpu.VMEM((256, 256), F32),
        ],
        values.reshape(SEQS, BLOCKS, 16, 128),
        filt,
        skip,
    )
    back = lax.all_to_all(conv.reshape(256, 16, 128), both, split_axis=0, concat_axis=0, tiled=True)
    experts = jnp.arange(64, dtype=I32)
    rep = (spare_pick[(experts // 2 + 16) % 32] == experts % 2).astype(F32)
    send, hidden = call(
        norm_kernel,
        (sds((HOMES, MSG, QW), BF16), sds((TOK, WIDTH), F32)),
        [pltpu.VMEM((TOK, WIDTH), BF16), pltpu.VMEM((64, TOK), F32)],
        back.reshape(HOMES, GROUPS, 16, 128),
        resid,
        gate_in,
        rims,
        gate_short,
        norm_gain.reshape(1, WIDTH),
        expert_ids.T,
        rep.reshape(64, 1),
    )
    recv = lax.all_to_all(send, "expert", split_axis=0, concat_axis=0, tiled=True)
    hot = lax.dynamic_slice_in_dim(spare_pick, (me + 16) % 32, 1, 0)
    outs = call(ffn_kernel, sds((HOMES, MSG, QW), BF16), [], hot, recv, w_gate, w_up, w_down, smem=1)
    ret = lax.all_to_all(outs, "expert", split_axis=0, concat_axis=0, tiled=True)
    return call(
        combine_kernel,
        sds((TOK, WIDTH), BF16),
        [pltpu.VMEM((2, TOK, HOMES * MAIN), BF16), pltpu.VMEM((2, TOK, HOMES * 16), BF16)],
        ret,
        hidden,
        expert_ids,
        gate_wts,
        rep.reshape(1, 64),
    )


def solution(mesh):
    placed = (
        P(("expert", "seq"), None),
        P(("expert", "seq"), None),
        P(),
        P(),
        P("expert", "seq"),
        P("seq"),
        P(),
        P(("expert", "seq"), None),
        P(("expert", "seq"), None),
        P(),
        P("expert", None, None),
        P("expert", None, None),
        P("expert", None, None),
    )
    return jax.shard_map(
        body, mesh=mesh, in_specs=placed, out_specs=P(("expert", "seq"), None), check_vma=False
    )
```

time: 457 us -> 288 us (0.63)
  the two profiles are of different devices: /device:TPU:40 before, /device:TPU:1 now
where the time goes in v1:
time: 288 us; the launch traced here: 285 us
  waiting for transfers between devices  182 us (63%)
  Pallas kernels  47.5 us (16%)
  starting transfers between devices  32.1 us (11%)
  blocking collectives  15 us (5%)
  local copies, waits for them, and re-layouts  7.25 us (3%)
    all_to_all x1, waiting for transfers between devices, body(): lax.all_to_all(send, 'expert', split_axis=0, concat_axis=0, tiled=True)  57.9 us
    all_to_all x1, waiting for transfers between devices, body(): lax.all_to_all(outs, 'expert', split_axis=0, concat_axis=0, tiled=True)  56.3 us
    pallas_call x5, Pallas kernels, call(): pl.pallas_call(kernel, out_shape=outs, in_specs=[pl.BlockSpec(memory_spac...  47.5 us
    all_to_all x1, waiting for transfers between devices, body(): lax.all_to_all(values.reshape(256, 16, 128), both, split_axis=0, concat_a...  31.4 us
    all_to_all x1, waiting for transfers between devices, body(): lax.all_to_all(conv.reshape(256, 16, 128), both, split_axis=0, concat_axi...  30.8 us
    all_to_all x1, blocking collectives, body(): lax.all_to_all(filt, 'expert', split_axis=0, concat_axis=0, tiled=True)  15 us
    all_to_all x1, starting transfers between devices, body(): lax.all_to_all(values.reshape(256, 16, 128), both, split_axis=0, concat_a...  8.79 us
    all_to_all x1, starting transfers between devices, body(): lax.all_to_all(outs, 'expert', split_axis=0, concat_axis=0, tiled=True)  7.75 us
  transfers between devices with their start and end apart: 5, of which 5 were waited for; matrix products, arithmetic and copies ran while one was open for 2% of the time, Pallas kernels for 0%

profile of v1, /device:TPU:1, one launch (start us, length us, event | category | flops | bytes accessed | tf_op | source)
XLA Modules:
  0.0 285.4 jit_solution(4339086150536780268)
XLA Ops:
  0.0 0.8 slice_bitcast_fusion
  0.8 4.4 %collective-permute-start = (bf16[2,2,2048]{2,1,0:T(2,128)(2,1)S(1)}, bf16[2,2,2048]{2,1,0:T(2,128)(2,1)S(1)}, u32[]{:S(2)}, u32[]{:S(2)}) collective-permute-start(bf16[2,2,2048]{2,1,0:T(2,128)(2,1)S(1)} %pad_maximum_fusion), channel_id=1, source_target_pairs={{0,1},{1,2},{2,3},{3,4},{4,5},{5,6},{6,7},{7,8},{8,9},{9,10},{10,1... | collective-permute-start | bytes 49160 | tf_op jit(solution)/shard_map/ppermute | solution.py:333
  5.2 5.9 %collective-permute-done = bf16[2,2,2048]{2,1,0:T(2,128)(2,1)S(1)} collective-permute-done((bf16[2,2,2048]{2,1,0:T(2,128)(2,1)S(1)}, bf16[2,2,2048]{2,1,0:T(2,128)(2,1)S(1)}, u32[]{:S(2)}, u32[]{:S(2)}) %collective-permute-start) | collective-permute-done | bytes 16416 | tf_op jit(solution)/shard_map/ppermute | solution.py:333
  11.2 0.6 reshape.168.rim_ref
  11.8 4.3 %shard_map.127 = (bf16[32,8,16,128]{3,2,1,0:T(8,128)(2,1)}, f32[32,8,128]{2,1,0:T(8,128)}) custom-call(bf16[256,2048]{1,0:T(8,128)(2,1)} %resid_ref.3, f32[4,2048]{1,0:T(4,128)} %reshape.168.rim_ref, f32[3,2048]{1,0:T(4,128)} %kern_ref.2, bf16[128,256]{1,0:T(8,128)(2,1)} %filt_ref.1), custom_call_target="tpu_custom_call" | custom-call | tf_op jit(solution)/shard_map/pallas_call | solution.py:302
  16.1 15.0 %all_to_all.25.filt_ref = f32[32,8,128]{2,1,0:T(8,128)} all-to-all(f32[32,8,128]{2,1,0:T(8,128)} %get-tuple-element.10), channel_id=1, replica_groups=mesh['expert'=32,'seq'=8] {'expert'}, dimensions={0} | all-to-all | bytes 262144 | tf_op jit(solution)/shard_map/all_to_all | solution.py:348
  31.1 8.8 %all-to-all-start = ((bf16[256,16,128]{2,1,0:T(8,128)(2,1)}), bf16[256,16,128]{2,1,0:T(8,128)(2,1)S(1)}, u32[]{:S(2)}, u32[]{:S(2)}) async-start(bf16[256,16,128]{2,1,0:T(8,128)(2,1)} %bitcast.19), calls=%async_computation | async-start | bytes 2097152 | tf_op jit(solution)/shard_map/all_to_all | solution.py:347
  39.9 0.8 dynamic_slice.7
  40.7 31.4 %all-to-all-done = bf16[256,16,128]{2,1,0:T(8,128)(2,1)S(1)} async-done(((bf16[256,16,128]{2,1,0:T(8,128)(2,1)}), bf16[256,16,128]{2,1,0:T(8,128)(2,1)S(1)}, u32[]{:S(2)}, u32[]{:S(2)}) %all-to-all-start) | async-done | bytes 1048608 | tf_op jit(solution)/shard_map/all_to_all | solution.py:347
  72.1 0.8 broadcast_in_dim.12.skip_ref
  72.9 0.2 copy-done.1
  73.1 10.5 %shard_map.128 = bf16[16,16,16,128]{3,2,1,0:T(8,128)(2,1)} custom-call(bf16[16,16,16,128]{3,2,1,0:T(8,128)(2,1)} %bitcast.16, f32[32,8,128]{2,1,0:T(8,128)} %all_to_all.25.filt_ref, f32[8,256]{1,0:T(8,128)} %broadcast_in_dim.12.skip_ref), custom_call_target="tpu_custom_call" | custom-call | tf_op jit(solution)/shard_map/pallas_call | solution.py:302
  83.6 5.9 %all-to-all-start.2 = ((bf16[256,16,128]{2,1,0:T(8,128)(2,1)}), bf16[256,16,128]{2,1,0:T(8,128)(2,1)S(1)}, u32[]{:S(2)}, u32[]{:S(2)}) async-start(bf16[256,16,128]{2,1,0:T(8,128)(2,1)} %bitcast.18), calls=%async_computation.2 | async-start | bytes 2097152 | tf_op jit(solution)/shard_map/all_to_all | solution.py:366
  89.5 0.0 copy-done
  89.5 0.8 gather_fusion
  90.3 0.1 copy.20
  90.4 0.6 convert_element_type.20.rep_ref
  91.0 30.8 %all-to-all-done.2 = bf16[256,16,128]{2,1,0:T(8,128)(2,1)S(1)} async-done(((bf16[256,16,128]{2,1,0:T(8,128)(2,1)}), bf16[256,16,128]{2,1,0:T(8,128)(2,1)S(1)}, u32[]{:S(2)}, u32[]{:S(2)}) %all-to-all-start.2) | async-done | bytes 1048608 | tf_op jit(solution)/shard_map/all_to_all | solution.py:366
  121.8 1.0 copy-done.2
  122.8 9.6 %shard_map.129 = (bf16[32,144,512]{2,1,0:T(8,128)(2,1)}, f32[256,2048]{1,0:T(8,128)}) custom-call(bf16[32,8,16,128]{3,2,1,0:T(8,128)(2,1)} %bitcast.17, bf16[256,2048]{1,0:T(8,128)(2,1)} %resid_ref.3, bf16[256,2048]{1,0:T(8,128)(2,1)} %gate_in_ref.1, f32[4,2048]{1,0:T(4,128)} %reshape.168.rim_ref, f32[3,2048]{1,0:T(4,128)} %kern_ref.3, f32[1,2048]{1,0:T(1,128)} %bitcast.21, ...), custom_call_target="tpu_custom_call" | custom-call | tf_op jit(solution)/shard_map/pallas_call | solution.py:302
  132.3 5.3 %all-to-all-start.3 = ((bf16[32,144,512]{2,1,0:T(8,128)(2,1)}), bf16[32,144,512]{2,1,0:T(8,128)(2,1)}, u32[]{:S(2)}, u32[]{:S(2)}) async-start(bf16[32,144,512]{2,1,0:T(8,128)(2,1)} %get-tuple-element.11), calls=%async_computation.3 | async-start | bytes 9437184 | tf_op jit(solution)/shard_map/all_to_all | solution.py:382
  137.7 0.6 dynamic_slice.6.hot_ref
  138.2 57.9 %all-to-all-done.3.recv_ref = bf16[32,144,512]{2,1,0:T(8,128)(2,1)} async-done(((bf16[32,144,512]{2,1,0:T(8,128)(2,1)}), bf16[32,144,512]{2,1,0:T(8,128)(2,1)}, u32[]{:S(2)}, u32[]{:S(2)}) %all-to-all-start.3) | async-done | bytes 4718624 | tf_op jit(solution)/shard_map/all_to_all | solution.py:382
  196.1 14.0 %shard_map.130 = bf16[32,144,512]{2,1,0:T(8,128)(2,1)} custom-call(s32[1]{0:T(128)} %dynamic_slice.6.hot_ref, bf16[32,144,512]{2,1,0:T(8,128)(2,1)} %all-to-all-done.3.recv_ref, bf16[2,2048,256]{2,1,0:T(8,128)(2,1)} %wg_ref.1, bf16[2,2048,256]{2,1,0:T(8,128)(2,1)} %wu_ref.1, bf16[2,2048,256]{2,1,0:T(8,128)(2,1)} %wd_ref.1), custom_call_target="tpu_custom_call" | custom-call | tf_op jit(solution)/shard_map/pallas_call | solution.py:302
  210.2 7.7 %all-to-all-start.4 = ((bf16[32,144,512]{2,1,0:T(8,128)(2,1)}), bf16[32,144,512]{2,1,0:T(8,128)(2,1)}, u32[]{:S(2)}, u32[]{:S(2)}) async-start(bf16[32,144,512]{2,1,0:T(8,128)(2,1)} %shard_map.130), calls=%async_computation.4 | async-start | bytes 9437184 | tf_op jit(solution)/shard_map/all_to_all | solution.py:385
  217.9 0.0 copy-done.3
  217.9 0.8 copy.21.ids_ref
  218.7 0.0 copy-done.4
  218.7 0.8 copy.22.wts_ref
  219.6 0.5 compare_convert_fusion.rep_ref
  220.1 56.3 %all-to-all-done.4.ret_ref = bf16[32,144,512]{2,1,0:T(8,128)(2,1)} async-done(((bf16[32,144,512]{2,1,0:T(8,128)(2,1)}), bf16[32,144,512]{2,1,0:T(8,128)(2,1)}, u32[]{:S(2)}, u32[]{:S(2)}) %all-to-all-start.4) | async-done | bytes 4718624 | tf_op jit(solution)/shard_map/all_to_all | solution.py:385
  276.3 9.1 %shard_map.131 = bf16[256,2048]{1,0:T(8,128)(2,1)} custom-call(bf16[32,144,512]{2,1,0:T(8,128)(2,1)} %all-to-all-done.4.ret_ref, f32[256,2048]{1,0:T(8,128)} %get-tuple-element.12.hid_ref, s32[256,4]{1,0:T(8,128)} %copy.21.ids_ref, f32[256,4]{1,0:T(8,128)} %copy.22.wts_ref, f32[1,64]{1,0:T(1,128)} %compare_convert_fusion.rep_ref), custom_call_target="tpu_custom_call" | custom-call | tf_op jit(solution)/shard_map/pallas_call | solution.py:302
  (10 shorter events, 0.1 us)
Async XLA Ops:
  0.0 89.5 %copy-start = (s32[32]{0:T(128)S(1)}, s32[32]{0:T(128)}, u32[]{:S(2)}) copy-start(s32[32]{0:T(128)} %param.22) | copy-start | bytes 388
  0.8 10.3 %collective-permute-start = (bf16[2,2,2048]{2,1,0:T(2,128)(2,1)S(1)}, bf16[2,2,2048]{2,1,0:T(2,128)(2,1)S(1)}, u32[]{:S(2)}, u32[]{:S(2)}) collective-permute-start(bf16[2,2,2048]{2,1,0:T(2,128)(2,1)S(1)} %pad_maximum_fusion), channel_id=1, source_target_pairs={{0,1},{1,2},{2,3},{3,4},{4,5},{5,6},{6,7},{7,8},{8,9},{9,10},{10,1... | collective-permute-start | bytes 49160 | tf_op jit(solution)/shard_map/ppermute | solution.py:333
  31.1 41.0 %all-to-all-start = ((bf16[256,16,128]{2,1,0:T(8,128)(2,1)}), bf16[256,16,128]{2,1,0:T(8,128)(2,1)S(1)}, u32[]{:S(2)}, u32[]{:S(2)}) async-start(bf16[256,16,128]{2,1,0:T(8,128)(2,1)} %bitcast.19), calls=%async_computation | async-start | bytes 2097152 | tf_op jit(solution)/shard_map/all_to_all | solution.py:347
  72.1 1.0 copy-start.1
  83.6 38.2 %all-to-all-start.2 = ((bf16[256,16,128]{2,1,0:T(8,128)(2,1)}), bf16[256,16,128]{2,1,0:T(8,128)(2,1)S(1)}, u32[]{:S(2)}, u32[]{:S(2)}) async-start(bf16[256,16,128]{2,1,0:T(8,128)(2,1)} %bitcast.18), calls=%async_computation.2 | async-start | bytes 2097152 | tf_op jit(solution)/shard_map/all_to_all | solution.py:366
  121.8 1.0 copy-start.2
  132.3 63.8 %all-to-all-start.3 = ((bf16[32,144,512]{2,1,0:T(8,128)(2,1)}), bf16[32,144,512]{2,1,0:T(8,128)(2,1)}, u32[]{:S(2)}, u32[]{:S(2)}) async-start(bf16[32,144,512]{2,1,0:T(8,128)(2,1)} %get-tuple-element.11), calls=%async_computation.3 | async-start | bytes 9437184 | tf_op jit(solution)/shard_map/all_to_all | solution.py:382
  210.2 7.8 %copy-start.3 = (s32[256,4]{0,1:T(4,128)S(1)}, s32[256,4]{0,1:T(4,128)}, u32[]{:S(2)}) copy-start(s32[256,4]{0,1:T(4,128)} %param.20) | copy-start | bytes 12292
  210.2 8.6 %copy-start.4 = (f32[256,4]{0,1:T(4,128)S(1)}, f32[256,4]{0,1:T(4,128)}, u32[]{:S(2)}) copy-start(f32[256,4]{0,1:T(4,128)} %param.21) | copy-start | bytes 12292
  210.2 66.2 %all-to-all-start.4 = ((bf16[32,144,512]{2,1,0:T(8,128)(2,1)}), bf16[32,144,512]{2,1,0:T(8,128)(2,1)}, u32[]{:S(2)}, u32[]{:S(2)}) async-start(bf16[32,144,512]{2,1,0:T(8,128)(2,1)} %shard_map.130), calls=%async_computation.4 | async-start | bytes 9437184 | tf_op jit(solution)/shard_map/all_to_all | solution.py:385

commit v2 on v1

v2 whole, which is shorter than its diff:
```python
import functools

import jax
import jax.numpy as jnp
from jax import lax
from jax.experimental import pallas as pl
from jax.experimental.pallas import tpu as pltpu
from jax.sharding import PartitionSpec as P

F32, BF16, I32 = jnp.float32, jnp.bfloat16, jnp.int32
VMEM_LIMIT = 56 * 1024 * 1024
TOK = 256
WIDTH = 2048
HOMES = 32
GROUPS = 8
SEQS = 16
BLOCKS = 16
CH = 8
POS = SEQS * TOK
QUARTERS = 4
QW = WIDTH // QUARTERS
MAIN = 32
LEFT = 4
MSG = QUARTERS * (MAIN + LEFT)
CAP = 12
HID = 256
PAD = 128
NEAR = HOMES * GROUPS
PARTS = 4
PER = HOMES // PARTS
MESH = pl.DeviceIdType.MESH


def iota(shape, dim):
    return lax.broadcasted_iota(I32, shape, dim)


def eye(n):
    return (iota((n, n), 0) == iota((n, n), 1)).astype(BF16)


def nt(a, b):
    return lax.dot_general(a, b, (((1,), (1,)), ((), ())), preferred_element_type=F32)


def mm(a, b):
    return jnp.dot(a, b, preferred_element_type=F32)


def short_conv(x, before2, before1, kernel):
    row = iota(x.shape, 0)
    back1 = jnp.where(row == 0, before1, pltpu.roll(x, 1, 0))
    back2 = jnp.where(row == 0, before2, jnp.where(row == 1, before1, pltpu.roll(x, 2, 0)))
    return kernel[0:1] * x + kernel[1:2] * back1 + kernel[2:3] * back2


def group_cols(g):
    return pl.ds(pl.multiple_of(g * 256, 256), 256)


def to_message(block):
    first = block[:, :128].reshape(32, 8, 128)
    second = block[:, 128:].reshape(32, 8, 128)
    return jnp.concatenate([first, second], axis=1).astype(BF16)


def from_message(message):
    wide = message.astype(F32)
    first = wide[:, :8].reshape(256, 128).astype(BF16)
    second = wide[:, 8:].reshape(256, 128).astype(BF16)
    ident = eye(128)
    return jnp.concatenate([nt(ident, first), nt(ident, second)], axis=0)


def build_bank(row, bank_ref):
    wide = jnp.concatenate([jnp.broadcast_to(row, (8, POS)), jnp.zeros((8, PAD), F32)], axis=1)
    base = pltpu.roll(wide, 0, 1, stride=1, stride_axis=0)
    for a in range(8):
        upper = pltpu.roll(base, 16 * a, 1) if a else base
        lower = pltpu.roll(base, 16 * a + 8, 1)
        both = jnp.concatenate([upper, lower], axis=0)[:, :POS].astype(BF16)
        bank_ref[16 * a : 16 * a + 16, :] = both
        bank_ref[128 + 16 * a : 144 + 16 * a, PAD:] = both[:, : POS - PAD]


def slots(named, rep, axis):
    tri = (iota((TOK, TOK), axis) < iota((TOK, TOK), 1 - axis)).astype(BF16)
    if axis == 0:
        rank = mm(named.astype(BF16), tri)
    else:
        rank = mm(tri, named.astype(BF16))
    kept = (named > 0) & ((rank < CAP) | ((rank < 2 * CAP) & (rep > 0)))
    return jnp.where(kept, jnp.where(rep > 0, rank, rank + 2 * CAP), -1.0)


def silu_mul(gate, up):
    return gate / (1.0 + jnp.exp(-gate)) * up


def ffn_group(first, n, recv_ref, wg_ref, wu_ref, wd_ref, out_ref, hot):
    cold = 1 - hot
    src = pl.ds(first, n)
    rows = 16 * n
    zero = functools.partial(jnp.zeros, (rows, HID), F32)
    ga, ua, gb, ub, gc, uc, gl, ul = (zero() for _ in range(8))
    left = recv_ref[src, MAIN * QUARTERS :, :].reshape(rows, QW)
    part = iota((rows, HID), 0) % 16 // 4
    for q in range(QUARTERS):
        xa = recv_ref[src, MAIN * q : MAIN * q + 16, :].reshape(rows, QW)
        xb = recv_ref[src, MAIN * q + 16 : MAIN * q + 32, :].reshape(rows, QW)
        cut = slice(QW * q, QW * q + QW)
        both = jnp.concatenate([xa, xb], axis=0)
        gh, uh = mm(both, wg_ref[hot, cut, :]), mm(both, wu_ref[hot, cut, :])
        ga, ua, gb, ub = ga + gh[:rows], ua + uh[:rows], gb + gh[rows:], ub + uh[rows:]
        both = jnp.concatenate([xb, left], axis=0)
        gh, uh = mm(both, wg_ref[cold, cut, :]), mm(both, wu_ref[cold, cut, :])
        gc, uc = gc + gh[:rows], uc + uh[:rows]
        gl = gl + jnp.where(part == q, gh[rows:], 0.0)
        ul = ul + jnp.where(part == q, uh[rows:], 0.0)

    def over_quarters(acc):
        acc = acc.reshape(n, 16, HID)
        acc = acc[:, :8] + acc[:, 8:]
        acc = acc.reshape(8 * n, HID)
        low = iota(acc.shape, 0) % 8 < 4
        other = jnp.where(low, pltpu.roll(acc, 8 * n - 4, 0), pltpu.roll(acc, 4, 0))
        acc = (acc + other).reshape(n, 8, HID)
        return jnp.concatenate([acc, acc], axis=1).reshape(rows, HID)

    is_hot = iota((rows, HID), 0) % 16 < 8
    act_a = silu_mul(ga, ua).astype(BF16)
    act_b = silu_mul(jnp.where(is_hot, gb, gc), jnp.where(is_hot, ub, uc))
    act_bh = jnp.where(is_hot, act_b, 0.0).astype(BF16)
    act_bc = jnp.where(is_hot, 0.0, act_b).astype(BF16)
    act_l = silu_mul(over_quarters(gl), over_quarters(ul)).astype(BF16)
    hot_in = jnp.concatenate([act_a, act_bh], axis=0)
    cold_in = jnp.concatenate([act_bc, act_l], axis=0)
    part = iota((rows, QW), 0) % 16 // 4
    spill = jnp.zeros((rows, QW), F32)
    for q in range(QUARTERS):
        cut = slice(QW * q, QW * q + QW)
        oh = nt(hot_in, wd_ref[hot, cut, :])
        oc = nt(cold_in, wd_ref[cold, cut, :])
        out_ref[src, MAIN * q : MAIN * q + 16, :] = oh[:rows].astype(BF16).reshape(n, 16, QW)
        out_ref[src, MAIN * q + 16 : MAIN * q + 32, :] = (oh[rows:] + oc[:rows]).astype(BF16).reshape(n, 16, QW)
        spill = jnp.where(part == q, oc[rows:], spill)
    out_ref[src, MAIN * QUARTERS :, :] = spill.astype(BF16).reshape(n, 16, QW)


def partner(order):
    t = (order + 1) * 11 % 32
    return 2 * (t % 2) + t // 2 % 2, 2 * (t // 4 % 2) + t // 8 % 2, t // 16


def ahead(e, offset, sign):
    dx, dy, dc = offset
    x = (e // 8 + 4 + sign * dx) % 4
    y = (e // 2 % 4 + 4 + sign * dy) % 4
    return 8 * x + 2 * y + (e + dc) % 2


def far(step):
    t = step * 37 % NEAR
    q = t // GROUPS
    return (q // 8, q // 2 % 4, q % 2), t % GROUPS


def exchange_kernel(
    resid_ref, rim_ref, kern_ref, filt_ref, skip_ref, out_ref,
    vsend, vrecv, fsend, frecv, csend, crecv, wide_ref, hrow_ref, x_ref, bank_ref, acc_ref,
    f_ssem, f_rsem, v_ssem, v_rsem, c_ssem, c_rsem,
):
    e, z = lax.axis_index("expert"), lax.axis_index("seq")
    barrier = pltpu.get_barrier_semaphore()

    def greet(step, _):
        offset, dz = far(step)
        target = (ahead(e, offset, 1), (z + dz) % GROUPS)
        pl.semaphore_signal(barrier, inc=1, device_id=target, device_id_type=MESH)
        return 0

    lax.fori_loop(1, NEAR, greet, 0)
    ident = eye(256)
    fsend[...] = nt(ident, filt_ref[...]).reshape(HOMES, CH, 128)

    def one(g, _):
        cols = group_cols(g)
        x = resid_ref[:, cols].astype(F32)
        values = short_conv(x, rim_ref[2:3, cols], rim_ref[3:4, cols], kern_ref[:, cols]).astype(BF16)
        vsend[g] = to_message(nt(ident, values))
        return 0

    lax.fori_loop(0, GROUPS, one, 0)
    pl.semaphore_wait(barrier, NEAR - 1)

    def send_filter(order, _):
        target = ahead(e, partner(order), 1)
        pltpu.make_async_remote_copy(
            src_ref=fsend.at[target], dst_ref=frecv.at[e], send_sem=f_ssem, recv_sem=f_rsem,
            device_id=(target, z), device_id_type=MESH,
        ).start()
        return 0

    lax.fori_loop(0, HOMES - 1, send_filter, 0)
    row = (e % 2 * GROUPS + z) * SEQS + e // 2

    def send_values(step, _):
        offset, dz = far(step)
        target, there = ahead(e, offset, 1), (z + dz) % GROUPS
        pltpu.make_async_remote_copy(
            src_ref=vsend.at[there, target], dst_ref=vrecv.at[row], send_sem=v_ssem, recv_sem=v_rsem,
            device_id=(target, there), device_id_type=MESH,
        ).start()
        return 0

    lax.fori_loop(1, NEAR, send_values, 0)
    frecv[e] = fsend[e]
    vrecv[row] = vsend[z, e]
    some = frecv.at[pl.ds(0, HOMES - 1)]
    pltpu.make_async_copy(some, some, f_rsem).wait()
    for d in range(HOMES):
        hrow_ref[:, 128 * d : 128 * d + 128] = frecv[d]
    bank_ref[:, 128:, :PAD] = jnp.zeros((CH, 128, PAD), BF16)

    def bank(c, _):
        build_bank(hrow_ref[pl.ds(c, 1), :], bank_ref.at[c])
        return 0

    lax.fori_loop(0, CH, bank, 0)
    some = vrecv.at[pl.ds(0, NEAR - 1)]
    pltpu.make_async_copy(some, some, v_rsem).wait()

    def widen(i, _):
        wide_ref[pl.ds(pl.multiple_of(i * 256, 256), 256)] = vrecv[pl.ds(i * 16, 16)].astype(F32).reshape(256, 128)
        return 0

    lax.fori_loop(0, BLOCKS, widen, 0)
    for c in range(CH):
        for half in range(2):
            x_ref[c, :, 128 * half : 128 * half + 128] = wide_ref[pl.ds(8 * half + c, 256, stride=16), :]

    def conv(c, _):
        x = x_ref[c]
        lhs = x.astype(BF16)
        acc_ref[...] = x * skip_ref[pl.ds(c, 1), :]
        for k in range(BLOCKS):
            acc_ref[16 * k :, :] += mm(lhs[: 256 - 16 * k], bank_ref[c, :, 256 * k : 256 * k + 256])
        x_ref[c] = acc_ref[...]
        return 0

    lax.fori_loop(0, CH, conv, 0)
    for c in range(CH):
        for half in range(2):
            wide_ref[pl.ds(8 * half + c, 256, stride=16), :] = x_ref[c, :, 128 * half : 128 * half + 128]

    def narrow(i, _):
        csend[pl.ds(i * 16, 16)] = wide_ref[pl.ds(pl.multiple_of(i * 256, 256), 256)].reshape(16, 16, 128).astype(BF16)
        return 0

    lax.fori_loop(0, BLOCKS, narrow, 0)

    def send_back(step, _):
        offset, dz = far(step)
        target, there = ahead(e, offset, 1), (z + dz) % GROUPS
        place = (target % 2 * GROUPS + there) * SEQS + target // 2
        pltpu.make_async_remote_copy(
            src_ref=csend.at[place], dst_ref=crecv.at[z, e], send_sem=c_ssem, recv_sem=c_rsem,
            device_id=(target, there), device_id_type=MESH,
        ).start()
        return 0

    lax.fori_loop(1, NEAR, send_back, 0)
    crecv[z, e] = csend[row]
    some = fsend.at[pl.ds(0, HOMES - 1)]
    pltpu.make_async_copy(some, some, f_ssem).wait()
    some = csend.at[pl.ds(0, NEAR - 1)]
    pltpu.make_async_copy(some, some, v_ssem).wait()
    pltpu.make_async_copy(some, some, c_rsem).wait()
    pltpu.make_async_copy(some, some, c_ssem).wait()
    out_ref[...] = crecv[...]


def prepare_weights(ids_ref, wts_ref, rep_ref, slot_ref, weight_ref):
    named = jnp.zeros((TOK, 64), F32)
    weight = jnp.zeros((TOK, 64), F32)
    for k in range(4):
        hit = ids_ref[:, k : k + 1] == iota((TOK, 64), 1)
        named += hit.astype(F32)
        weight += jnp.where(hit, wts_ref[:, k : k + 1], 0.0)
    slot_ref[...] = slots(named, rep_ref[...], 1).astype(BF16)
    high = weight.astype(BF16)
    weight_ref[0] = high
    weight_ref[1] = (weight - high.astype(F32)).astype(BF16)


def part_weights(e, g, per, want, slot_ref, weight_ref):
    shape = (64, PER * per)
    home = ahead(e, partner(PER * g + iota(shape, 1) // per), 1)
    high = low = jnp.zeros((TOK, PER * per), F32)
    for odd in range(2):
        pick = (iota(shape, 0) == 2 * home + odd).astype(BF16)
        hit = mm(slot_ref[...], pick) == want
        high = high + jnp.where(hit, mm(weight_ref[0], pick), 0.0)
        low = low + jnp.where(hit, mm(weight_ref[1], pick), 0.0)
    return high.astype(BF16), low.astype(BF16)


def experts_kernel(
    hot_ref, back_ref, resid_ref, gate_in_ref, rim_ref, kern_ref, gain_ref, idst_ref, ids_ref, wts_ref, repc_ref, repr_ref,
    wg_ref, wu_ref, wd_ref, out_ref,
    hid_ref, normed_ref, slott_ref, slot_ref, weight_ref, wmain_ref, wleft_ref, send, recv, give, ret,
    d_ssem, d_rsem, r_ssem, r_rsem,
):
    e, z = lax.axis_index("expert"), lax.axis_index("seq")
    barrier = pltpu.get_barrier_semaphore()

    def greet(order, _):
        target = (ahead(e, partner(order), 1), z)
        pl.semaphore_signal(barrier, inc=1, device_id=target, device_id_type=MESH)
        return 0

    lax.fori_loop(0, HOMES - 1, greet, 0)

    def one(g, total):
        cols = group_cols(g)
        x = gate_in_ref[:, cols].astype(F32)
        gated = short_conv(x, rim_ref[0:1, cols], rim_ref[1:2, cols], kern_ref[:, cols])
        hidden = resid_ref[:, cols].astype(F32) + gated * from_message(back_ref[g])
        hid_ref[:, cols] = hidden
        return total + jnp.sum(hidden * hidden, axis=1, keepdims=True)

    total = lax.fori_loop(0, GROUPS, one, jnp.zeros((TOK, 1), F32))
    scale = lax.rsqrt(total * (1.0 / WIDTH) + 1e-05)

    def two(g, _):
        cols = group_cols(g)
        normed_ref[:, cols] = (hid_ref[:, cols] * scale * gain_ref[:, cols]).astype(BF16)
        return 0

    lax.fori_loop(0, GROUPS, two, 0)
    named = jnp.zeros((64, TOK), F32)
    for k in range(4):
        named += (idst_ref[k : k + 1, :] == iota((64, TOK), 0)).astype(F32)
    slott_ref[...] = slots(named, repc_ref[...], 0)
    pl.semaphore_wait(barrier, HOMES - 1)

    def move(source, sink, order, sign, ssem, rsem):
        pltpu.make_async_remote_copy(
            src_ref=source.at[order], dst_ref=sink.at[order], send_sem=ssem, recv_sem=rsem,
            device_id=(ahead(e, partner(order), sign), z), device_id_type=MESH,
        ).start()

    def move_part(source, sink, g, sign, ssem, rsem):
        for j in range(PER - 1):
            move(source, sink, PER * g + j, sign, ssem, rsem.at[g])

        @pl.when(g < PARTS - 1)
        def _():
            move(source, sink, PER * g + PER - 1, sign, ssem, rsem.at[g])

        @pl.when(g == PARTS - 1)
        def _():
            pltpu.make_async_copy(source.at[HOMES - 1], sink.at[HOMES - 1], rsem.at[g]).start()

    def wait_part(sink, g, rsem):
        part = sink.at[pl.ds(PER * g, PER)]
        pltpu.make_async_copy(part, part, rsem.at[g]).wait()

    def dispatch(g, _):
        sel = []
        left = []
        for j in range(PER):
            home = ahead(e, partner(PER * g + j), 1)
            even = slott_ref[pl.ds(2 * home, 1), :]
            odd = slott_ref[pl.ds(2 * home + 1, 1), :]
            r = iota((MAIN, TOK), 0).astype(F32)
            sel.append(((even == r) | (odd == r)).astype(BF16))
            r = (iota((16, TOK), 0) % 4 + MAIN).astype(F32)
            left.append(((even == r) | (odd == r)).astype(F32))
        sel = jnp.concatenate(sel, axis=0)
        left = jnp.concatenate(left, axis=0)
        part = iota((16 * PER, TOK), 0) % 16 // 4
        spill = jnp.zeros((16 * PER, QW), F32)
        for q in range(QUARTERS):
            cols = normed_ref[:, QW * q : QW * q + QW]
            send[pl.ds(PER * g, PER), MAIN * q : MAIN * q + MAIN, :] = mm(sel, cols).astype(BF16).reshape(PER, MAIN, QW)
            spill += mm(jnp.where(part == q, left, 0.0).astype(BF16), cols)
        send[pl.ds(PER * g, PER), MAIN * QUARTERS :, :] = spill.astype(BF16).reshape(PER, 16, QW)
        move_part(send, recv, g, 1, d_ssem, d_rsem)
        return 0

    lax.fori_loop(0, PARTS, dispatch, 0)
    prepare_weights(ids_ref, wts_ref, repr_ref, slot_ref, weight_ref)

    def weigh(g, _):
        want = (iota((TOK, PER * MAIN), 1) % MAIN).astype(F32)
        wmain_ref[g, 0], wmain_ref[g, 1] = part_weights(e, g, MAIN, want, slot_ref, weight_ref)
        want = (iota((TOK, PER * 16), 1) % 4 + MAIN).astype(F32)
        wleft_ref[g, 0], wleft_ref[g, 1] = part_weights(e, g, 16, want, slot_ref, weight_ref)
        return 0

    lax.fori_loop(0, PARTS, weigh, 0)
    hot = hot_ref[0]

    def expert(g, _):
        wait_part(recv, g, d_rsem)
        ffn_group(PER * g, PER, recv, wg_ref, wu_ref, wd_ref, give, hot)
        move_part(give, ret, g, -1, r_ssem, r_rsem)
        return 0

    lax.fori_loop(0, PARTS, expert, 0)

    def combine(g, _):
        wait_part(ret, g, r_rsem)
        left = ret[pl.ds(PER * g, PER), MAIN * QUARTERS :, :].reshape(PER * 16, QW)
        part = iota((TOK, PER * 16), 1) % 16 // 4
        for q in range(QUARTERS):
            main = ret[pl.ds(PER * g, PER), MAIN * q : MAIN * q + MAIN, :].reshape(PER * MAIN, QW)
            moe = mm(wmain_ref[g, 0], main) + mm(wmain_ref[g, 1], main)
            for w in range(2):
                moe += mm(jnp.where(part == q, wleft_ref[g, w].astype(F32), 0.0).astype(BF16), left)
            cut = slice(QW * q, QW * q + QW)
            hid_ref[:, cut] += moe
        return 0

    lax.fori_loop(0, PARTS, combine, 0)
    some = send.at[pl.ds(0, HOMES - 1)]
    pltpu.make_async_copy(some, some, d_ssem).wait()
    pltpu.make_async_copy(some, some, r_ssem).wait()
    out_ref[...] = hid_ref[...].astype(BF16)


def whole(n):
    return [pl.BlockSpec(memory_space=pltpu.VMEM)] * n


def call(kernel, outs, scratch, *args, cid, smem=0):
    return pl.pallas_call(
        kernel,
        out_shape=outs,
        in_specs=[pl.BlockSpec(memory_space=pltpu.SMEM)] * smem + whole(len(args) - smem),
        out_specs=whole(1)[0] if not isinstance(outs, tuple) else tuple(whole(len(outs))),
        scratch_shapes=scratch,
        compiler_params=pltpu.CompilerParams(
            vmem_limit_bytes=VMEM_LIMIT, collective_id=cid, has_side_effects=True
        ),
    )(*args)


def body(
    resid,
    gate_in,
    gate_short,
    value_short,
    long_filter,
    skip_gain,
    norm_gain,
    expert_ids,
    gate_wts,
    spare_pick,
    w_gate,
    w_up,
    w_down,
):
    n_seq = lax.axis_size("seq")
    n_exp = lax.axis_size("expert")
    me = lax.axis_index("expert")
    z = lax.axis_index("seq")
    tails = jnp.stack([gate_in[-2:], resid[-2:]])
    count = n_exp * n_seq
    rims = lax.ppermute(tails, ("expert", "seq"), [(i, i + 1) for i in range(count - 1)])
    rims = jnp.where((z == 0) & (me % 2 == 0), jnp.zeros((), BF16), rims)
    rims = rims.astype(F32).reshape(4, WIDTH)
    sds = jax.ShapeDtypeStruct
    skip = lax.dynamic_slice_in_dim(skip_gain, me * CH, CH, 0)
    skip = jnp.broadcast_to(skip[:, None], (CH, 256))
    experts = jnp.arange(64, dtype=I32)
    rep = (spare_pick[(experts // 2 + 16) % 32] == experts % 2).astype(F32)
    hot = lax.dynamic_slice_in_dim(spare_pick, (me + 16) % 32, 1, 0)
    dma = pltpu.SemaphoreType.DMA
    back = call(
        exchange_kernel,
        sds((GROUPS, HOMES, 16, 128), BF16),
        [
            pltpu.VMEM((GROUPS, HOMES, 16, 128), BF16),
            pltpu.VMEM((NEAR, 16, 128), BF16),
            pltpu.VMEM((HOMES, CH, 128), F32),
            pltpu.VMEM((HOMES, CH, 128), F32),
            pltpu.VMEM((NEAR, 16, 128), BF16),
            pltpu.VMEM((GROUPS, HOMES, 16, 128), BF16),
            pltpu.VMEM((POS, 128), F32),
            pltpu.VMEM((CH, POS), F32),
            pltpu.VMEM((CH, 256, 256), F32),
            pltpu.VMEM((CH, 256, POS), BF16),
            pltpu.VMEM((256, 256), F32),
        ]
        + [dma] * 6,
        resid,
        rims,
        value_short,
        long_filter,
        skip,
        cid=0,
    )
    message = pltpu.VMEM((HOMES, MSG, QW), BF16)
    return call(
        experts_kernel,
        sds((TOK, WIDTH), BF16),
        [
            pltpu.VMEM((TOK, WIDTH), F32),
            pltpu.VMEM((TOK, WIDTH), BF16),
            pltpu.VMEM((64, TOK), F32),
            pltpu.VMEM((TOK, 64), BF16),
            pltpu.VMEM((2, TOK, 64), BF16),
            pltpu.VMEM((PARTS, 2, TOK, PER * MAIN), BF16),
            pltpu.VMEM((PARTS, 2, TOK, PER * 16), BF16),
            message,
            message,
            message,
            message,
            dma,
            dma((PARTS,)),
            dma,
            dma((PARTS,)),
        ],
        hot,
        back,
        resid,
        gate_in,
        rims,
        gate_short,
        norm_gain.reshape(1, WIDTH),
        expert_ids.T,
        expert_ids,
        gate_wts,
        rep.reshape(64, 1),
        rep.reshape(1, 64),
        w_gate,
        w_up,
        w_down,
        smem=1,
        cid=1,
    )


def solution(mesh):
    placed = (
        P(("expert", "seq"), None),
        P(("expert", "seq"), None),
        P(),
        P(),
        P("expert", "seq"),
        P("seq"),
        P(),
        P(("expert", "seq"), None),
        P(("expert", "seq"), None),
        P(),
        P("expert", None, None),
        P("expert", None, None),
        P("expert", None, None),
    )
    return jax.shard_map(
        body, mesh=mesh, in_specs=placed, out_specs=P(("expert", "seq"), None), check_vma=False
    )
```

time: 288 us -> 249 us (0.86)
  the two profiles are of different devices: /device:TPU:1 before, /device:TPU:53 now
where the time goes in v2:
time: 249 us
  Pallas kernels  233 us (94%)
  local copies, waits for them, and re-layouts  10.9 us (4%)
  starting transfers between devices  3.55 us (1%)
    pallas_call x2, Pallas kernels, call(): pl.pallas_call(kernel, out_shape=outs, in_specs=[pl.BlockSpec(memory_spac...  233 us
    unnamed x3, local copies, waits for them, and re-layouts  5.27 us
  transfers between devices with their start and end apart: 1, of which 0 were waited for; matrix products, arithmetic and copies ran while one was open for 3% of the time, Pallas kernels for 0%

profile of v2, /device:TPU:53, one launch (start us, length us, event | category | flops | bytes accessed | tf_op | source)
XLA Modules:
  0.0 248.5 jit_solution(11469005276490240028)
XLA Ops:
  0.0 0.8 slice_bitcast_fusion
  0.8 3.5 %collective-permute-start = (bf16[2,2,2048]{2,1,0:T(2,128)(2,1)S(1)}, bf16[2,2,2048]{2,1,0:T(2,128)(2,1)S(1)}, u32[]{:S(2)}, u32[]{:S(2)}) collective-permute-start(bf16[2,2,2048]{2,1,0:T(2,128)(2,1)S(1)} %pad_maximum_fusion), channel_id=1, source_target_pairs={{0,1},{1,2},{2,3},{3,4},{4,5},{5,6},{6,7},{7,8},{8,9},{9,10},{10,1... | collective-permute-start | bytes 49160 | tf_op jit(solution)/shard_map/ppermute | solution.py:471
  4.4 1.4 gather_fusion
  5.9 0.6 compare_convert_fusion.repr_ref
  6.4 1.3 dynamic_slice.6.hot_ref
  7.7 0.1 copy.20
  7.8 0.6 convert_element_type.20.repc_ref
  8.4 1.5 copy.22.wts_ref
  9.9 1.5 copy.21.ids_ref
  11.4 0.8 dynamic_slice.7
  12.1 0.0 collective-permute-done
  12.1 0.6 reshape.152.rim_ref
  12.8 0.7 broadcast_in_dim.12.skip_ref
  13.4 83.8 %shard_map.127.back_ref = bf16[8,32,16,128]{3,2,1,0:T(8,128)(2,1)} custom-call(bf16[256,2048]{1,0:T(8,128)(2,1)} %resid_ref.3, f32[4,2048]{1,0:T(4,128)} %reshape.152.rim_ref, f32[3,2048]{1,0:T(4,128)} %kern_ref.2, bf16[128,256]{1,0:T(8,128)(2,1)} %filt_ref.1, f32[8,256]{1,0:T(8,128)} %broadcast_in_dim.12.skip_ref), custom_call_target="tpu_custom_call" | custom-call | tf_op jit(solution)/shard_map/pallas_call | solution.py:438
  97.3 148.9 %shard_map.128 = bf16[256,2048]{1,0:T(8,128)(2,1)} custom-call(s32[1]{0:T(128)} %dynamic_slice.6.hot_ref, bf16[8,32,16,128]{3,2,1,0:T(8,128)(2,1)} %shard_map.127.back_ref, bf16[256,2048]{1,0:T(8,128)(2,1)} %resid_ref.3, bf16[256,2048]{1,0:T(8,128)(2,1)} %gate_in_ref.1, f32[4,2048]{1,0:T(4,128)} %reshape.152.rim_ref, f32[3,2048]{1,0:T(4,128)} %kern_ref.3, ...), custom_call_target="tpu_custom_call" | custom-call | tf_op jit(solution)/shard_map/pallas_call | solution.py:438
  246.2 2.3 copy.24
  (5 shorter events, 0.1 us)
Async XLA Ops:
  0.8 11.3 %collective-permute-start = (bf16[2,2,2048]{2,1,0:T(2,128)(2,1)S(1)}, bf16[2,2,2048]{2,1,0:T(2,128)(2,1)S(1)}, u32[]{:S(2)}, u32[]{:S(2)}) collective-permute-start(bf16[2,2,2048]{2,1,0:T(2,128)(2,1)S(1)} %pad_maximum_fusion), channel_id=1, source_target_pairs={{0,1},{1,2},{2,3},{3,4},{4,5},{5,6},{6,7},{7,8},{8,9},{9,10},{10,1... | collective-permute-start | bytes 49160 | tf_op jit(solution)/shard_map/ppermute | solution.py:471

commit v3 on v2

v3 whole, which is shorter than its diff:
```python
import functools

import jax
import jax.numpy as jnp
from jax import lax
from jax.experimental import pallas as pl
from jax.experimental.pallas import tpu as pltpu
from jax.sharding import PartitionSpec as P

F32, BF16, I32 = jnp.float32, jnp.bfloat16, jnp.int32
VMEM_LIMIT = 60 * 1024 * 1024
TOK = 256
WIDTH = 2048
HOMES = 32
GROUPS = 8
SEQS = 16
BLOCKS = 16
CH = 8
POS = SEQS * TOK
QUARTERS = 4
QW = WIDTH // QUARTERS
MAIN = 32
LEFT = 4
MSG = QUARTERS * (MAIN + LEFT)
CAP = 12
HID = 256
PAD = 128
NEAR = HOMES * GROUPS
PARTS = 4
PER = HOMES // PARTS
MESH = pl.DeviceIdType.MESH


def iota(shape, dim):
    return lax.broadcasted_iota(I32, shape, dim)


def eye(n):
    return (iota((n, n), 0) == iota((n, n), 1)).astype(BF16)


def nt(a, b):
    return lax.dot_general(a, b, (((1,), (1,)), ((), ())), preferred_element_type=F32)


def mm(a, b):
    return jnp.dot(a, b, preferred_element_type=F32)


def short_conv(x, before2, before1, kernel):
    row = iota(x.shape, 0)
    back1 = jnp.where(row == 0, before1, pltpu.roll(x, 1, 0))
    back2 = jnp.where(row == 0, before2, jnp.where(row == 1, before1, pltpu.roll(x, 2, 0)))
    return kernel[0:1] * x + kernel[1:2] * back1 + kernel[2:3] * back2


def group_cols(g):
    return pl.ds(pl.multiple_of(g * 256, 256), 256)


def to_message(block):
    first = block[:, :128].reshape(32, 8, 128)
    second = block[:, 128:].reshape(32, 8, 128)
    return jnp.concatenate([first, second], axis=1).astype(BF16)


def from_message(message):
    wide = message.astype(F32)
    first = wide[:, :8].reshape(256, 128).astype(BF16)
    second = wide[:, 8:].reshape(256, 128).astype(BF16)
    ident = eye(128)
    return jnp.concatenate([nt(ident, first), nt(ident, second)], axis=0)


def partner(order):
    t = (order + 1) * 11 % 32
    return 2 * (t % 2) + t // 2 % 2, 2 * (t // 4 % 2) + t // 8 % 2, t // 16


def ahead(e, offset, sign):
    dx, dy, dc = offset
    x = (e // 8 + 4 + sign * dx) % 4
    y = (e // 2 % 4 + 4 + sign * dy) % 4
    return 8 * x + 2 * y + (e + dc) % 2


def slots(named, rep, axis):
    tri = (iota((TOK, TOK), axis) < iota((TOK, TOK), 1 - axis)).astype(BF16)
    if axis == 0:
        rank = mm(named.astype(BF16), tri)
    else:
        rank = mm(tri, named.astype(BF16))
    kept = (named > 0) & ((rank < CAP) | ((rank < 2 * CAP) & (rep > 0)))
    return jnp.where(kept, jnp.where(rep > 0, rank, rank + 2 * CAP), -1.0)


def prepare_routing(spare_ref, idst_ref, wtst_ref, slott_ref, slot_ref, weight_ref):
    expert, index = iota((64, HOMES), 0), iota((64, HOMES), 1)
    picked = jnp.where(index == (expert // 2 + 16) % 32, spare_ref[...], 0)
    rep = jnp.sum(picked.astype(F32), axis=1, keepdims=True) == (iota((64, 1), 0) % 2).astype(F32)
    named = jnp.zeros((64, TOK), F32)
    weight = jnp.zeros((64, TOK), F32)
    for k in range(4):
        hit = idst_ref[k : k + 1, :] == iota((64, TOK), 0)
        named += hit.astype(F32)
        weight += jnp.where(hit, wtst_ref[k : k + 1, :], 0.0)
    slot = slots(named, rep.astype(F32), 0)
    slott_ref[...] = slot
    ident = eye(TOK)
    slot_ref[...] = nt(ident, slot.astype(BF16)).astype(BF16)
    high = weight.astype(BF16)
    weight_ref[0] = nt(ident, high).astype(BF16)
    weight_ref[1] = nt(ident, (weight - high.astype(F32)).astype(BF16)).astype(BF16)


def part_picks(e, g, per):
    shape = (64, PER * per)
    home = ahead(e, partner(PER * g + iota(shape, 1) // per), 1)
    return [(iota(shape, 0) == 2 * home + odd).astype(BF16) for odd in range(2)]


def part_hits(e, g, per, want, slot_ref):
    return [mm(slot_ref[...], pick) == want for pick in part_picks(e, g, per)]


def part_weights(e, g, per, want, slot_ref, weight_ref):
    high = low = jnp.zeros((TOK, PER * per), F32)
    for pick in part_picks(e, g, per):
        hit = mm(slot_ref[...], pick) == want
        high = high + jnp.where(hit, mm(weight_ref[0], pick), 0.0)
        low = low + jnp.where(hit, mm(weight_ref[1], pick), 0.0)
    return high.astype(BF16), low.astype(BF16)


def build_bank(row, bank_ref):
    wide = jnp.concatenate([jnp.broadcast_to(row, (8, POS)), jnp.zeros((8, PAD), F32)], axis=1)
    base = pltpu.roll(wide, 0, 1, stride=1, stride_axis=0)
    for a in range(8):
        upper = pltpu.roll(base, 16 * a, 1) if a else base
        lower = pltpu.roll(base, 16 * a + 8, 1)
        both = jnp.concatenate([upper, lower], axis=0)[:, :POS].astype(BF16)
        bank_ref[16 * a : 16 * a + 16, PAD:] = both


def arrival(i):
    return jnp.where(i % 2 == 1, (i + 1) // 2, GROUPS - i // 2) % GROUPS


def silu_mul(gate, up):
    return gate / (1.0 + jnp.exp(-gate)) * up


def scale_columns(g, scales, lanes_of, per):
    cols = []
    for j in range(PER):
        sub, lane, rows = lanes_of(j)
        line = scales[PER * g + j, sub : sub + 1, :]
        hit = iota((per, 128), 1) == lane + iota((per, 128), 0)
        cols.append(jnp.sum(jnp.where(hit, line, 0.0), axis=1, keepdims=True))
    return jnp.concatenate(cols, axis=0)


def ffn_group(g, groups, scales, recv_ref, wg_ref, wu_ref, wd_ref, out_ref, hot):
    cold = 1 - hot
    n = PER
    src = pl.ds(g * PER, n)
    rows = 16 * n
    zero = functools.partial(jnp.zeros, (rows, HID), F32)
    ga, ua, gb, ub, gc, uc, gl, ul = (zero() for _ in range(8))
    part = iota((rows, HID), 0) % 16 // 4
    for i in range(GROUPS):
        q = i // 2
        lanes = slice(256 * (i % 2), 256 * (i % 2) + 256)
        xa = recv_ref[src, MAIN * q : MAIN * q + 16, lanes].reshape(rows, 256)
        xb = recv_ref[src, MAIN * q + 16 : MAIN * q + 32, lanes].reshape(rows, 256)
        left = recv_ref[src, MAIN * QUARTERS :, lanes].reshape(rows, 256)
        cut = group_cols(groups[i])
        both = jnp.concatenate([xa, xb], axis=0)
        gh, uh = mm(both, wg_ref[hot, cut, :]), mm(both, wu_ref[hot, cut, :])
        ga, ua, gb, ub = ga + gh[:rows], ua + uh[:rows], gb + gh[rows:], ub + uh[rows:]
        both = jnp.concatenate([xb, left], axis=0)
        gh, uh = mm(both, wg_ref[cold, cut, :]), mm(both, wu_ref[cold, cut, :])
        gc, uc = gc + gh[:rows], uc + uh[:rows]
        gl = gl + jnp.where(part == q, gh[rows:], 0.0)
        ul = ul + jnp.where(part == q, uh[rows:], 0.0)

    def over_quarters(acc):
        acc = acc.reshape(n, 16, HID)
        acc = acc[:, :8] + acc[:, 8:]
        acc = acc.reshape(8 * n, HID)
        low = iota(acc.shape, 0) % 8 < 4
        other = jnp.where(low, pltpu.roll(acc, 8 * n - 4, 0), pltpu.roll(acc, 4, 0))
        acc = (acc + other).reshape(n, 8, HID)
        return jnp.concatenate([acc, acc], axis=1).reshape(rows, HID)

    sa = scale_columns(g, scales, lambda j: (j // 4, 32 * (j % 4), 16), 16)
    sb = scale_columns(g, scales, lambda j: (j // 4, 32 * (j % 4) + 16, 16), 16)
    sl = scale_columns(g, scales, lambda j: (2, 16 * j, 16), 16)
    is_hot = iota((rows, HID), 0) % 16 < 8
    act_a = silu_mul(ga * sa, ua * sa).astype(BF16)
    act_b = silu_mul(jnp.where(is_hot, gb, gc) * sb, jnp.where(is_hot, ub, uc) * sb)
    act_bh = jnp.where(is_hot, act_b, 0.0).astype(BF16)
    act_bc = jnp.where(is_hot, 0.0, act_b).astype(BF16)
    act_l = silu_mul(over_quarters(gl) * sl, over_quarters(ul) * sl).astype(BF16)
    hot_in = jnp.concatenate([act_a, act_bh], axis=0)
    cold_in = jnp.concatenate([act_bc, act_l], axis=0)
    part = iota((rows, 256), 0) % 16 // 4
    spill = [jnp.zeros((rows, 256), F32)] * 2
    for i in range(GROUPS):
        q = i // 2
        lanes = slice(256 * (i % 2), 256 * (i % 2) + 256)
        cut = group_cols(groups[i])
        oh = nt(hot_in, wd_ref[hot, cut, :])
        oc = nt(cold_in, wd_ref[cold, cut, :])
        out_ref[src, MAIN * q : MAIN * q + 16, lanes] = oh[:rows].astype(BF16).reshape(n, 16, 256)
        out_ref[src, MAIN * q + 16 : MAIN * q + 32, lanes] = (oh[rows:] + oc[:rows]).astype(BF16).reshape(n, 16, 256)
        spill[i % 2] = jnp.where(part == q, oc[rows:], spill[i % 2])
    out_ref[src, MAIN * QUARTERS :, :] = jnp.concatenate(spill, axis=1).astype(BF16).reshape(n, 16, QW)


def layer_kernel(
    spare_ref, skip_ref, resid_ref, gate_in_ref, gate_kern_ref, value_kern_ref, filt_ref, gain_ref, idst_ref, wtst_ref,
    row_ref, wg_hbm, wu_hbm, wd_hbm, out_ref,
    vsend, vrecv, fsend, frecv, csend, crecv, rims, wide_ref, hrow_ref, x_ref, bank_ref, acc_ref,
    hid_ref, normed_ref, slott_ref, slot_ref, weight_ref, sel_ref, left_ref, wmain_ref, wleft_ref,
    send, recv, give, ret, ssend, srecv, wg_ref, wu_ref, wd_ref,
    b_sem, w_sem, t_ssem, t_rsem, f_ssem, f_rsem, v_ssem, v_rsem, c_ssem, c_rsem, s_ssem, s_rsem, d_ssem, d_rsem, r_ssem, r_rsem,
):
    e, z = lax.axis_index("expert"), lax.axis_index("seq")

    def device(order, sign=1):
        return ahead(e, partner(order), sign)

    def remote(source, sink, ssem, rsem, expert, seq):
        pltpu.make_async_remote_copy(
            src_ref=source, dst_ref=sink, send_sem=ssem, recv_sem=rsem, device_id=(expert, seq), device_id_type=MESH
        ).start()

    def await_bytes(ref, sem):
        pltpu.make_async_copy(ref, ref, sem).wait()

    barrier = pltpu.get_barrier_semaphore()

    def greet_line(dz, _):
        pl.semaphore_signal(barrier, inc=1, device_id=(e, (z + dz) % GROUPS), device_id_type=MESH)
        return 0

    def greet_plane(order, _):
        pl.semaphore_signal(barrier, inc=1, device_id=(device(order), z), device_id_type=MESH)
        return 0

    lax.fori_loop(1, GROUPS, greet_line, 0)
    lax.fori_loop(0, HOMES - 1, greet_plane, 0)
    weights = [
        pltpu.make_async_copy(hbm, vmem, w_sem.at[i])
        for i, (hbm, vmem) in enumerate(((wg_hbm, wg_ref), (wu_hbm, wu_ref), (wd_hbm, wd_ref)))
    ]
    for copy in weights:
        copy.start()
    ident = eye(256)
    fsend[...] = nt(ident, filt_ref[...]).reshape(HOMES, CH, 128)
    pl.semaphore_wait(barrier, GROUPS - 1 + HOMES - 1)

    def greet_again(dz, _):
        pl.semaphore_signal(b_sem, inc=1, device_id=(e, (z + dz) % GROUPS), device_id_type=MESH)
        return 0

    lax.fori_loop(1, GROUPS, greet_again, 0)
    pl.semaphore_wait(b_sem, GROUPS - 1)

    following = ((e + (z + 1) // GROUPS) % HOMES, (z + 1) % GROUPS)
    remote(gate_in_ref.at[pl.ds(TOK - 16, 16)], rims.at[0], t_ssem.at[0], t_rsem.at[0], *following)
    remote(resid_ref.at[pl.ds(TOK - 16, 16)], rims.at[1], t_ssem.at[1], t_rsem.at[1], *following)

    def send_filter(order, _):
        target = device(order)
        remote(fsend.at[target], frecv.at[e], f_ssem, f_rsem, target, z)
        return 0

    lax.fori_loop(0, HOMES - 1, send_filter, 0)
    frecv[e] = fsend[e]
    at_start = (z == 0) & (e % 2 == 0)

    def branch(ref, which, cols, kernel):
        tail = rims[which, :, cols].astype(F32)
        tail = jnp.where(at_start, 0.0, tail)
        return short_conv(ref[:, cols].astype(F32), tail[14:15], tail[15:16], kernel)

    await_bytes(rims.at[0], t_rsem.at[0])
    await_bytes(rims.at[1], t_rsem.at[1])
    row = (e % 2 * GROUPS + z) * SEQS + e // 2

    def make_values(r, _):
        there = (z + 3 * r + 4) % GROUPS
        cols = group_cols(there)
        values = branch(resid_ref, 1, cols, value_kern_ref[:, cols]).astype(BF16)
        vsend[there] = to_message(nt(ident, values))

        def send_values(order, _):
            target = device(order)
            remote(vsend.at[there, target], vrecv.at[row], v_ssem, v_rsem, target, there)
            return 0

        lax.fori_loop(0, HOMES - 1, send_values, 0)

        @pl.when(there != z)
        def _():
            remote(vsend.at[there, e], vrecv.at[row], v_ssem, v_rsem, e, there)

        return 0

    lax.fori_loop(0, GROUPS, make_values, 0)
    vrecv[row] = vsend[z, e]

    await_bytes(frecv.at[pl.ds(0, HOMES - 1)], f_rsem)
    for d in range(HOMES):
        hrow_ref[:, 128 * d : 128 * d + 128] = frecv[d]
    bank_ref[:, :, :PAD] = jnp.zeros((CH, 128, PAD), BF16)

    def bank(c, _):
        build_bank(hrow_ref[pl.ds(c, 1), :], bank_ref.at[c])
        return 0

    lax.fori_loop(0, CH, bank, 0)
    prepare_routing(row_ref, idst_ref, wtst_ref, slott_ref, slot_ref, weight_ref)

    def select(g, _):
        sel = []
        left = []
        for j in range(PER):
            home = device(PER * g + j)
            even = slott_ref[pl.ds(2 * home, 1), :]
            odd = slott_ref[pl.ds(2 * home + 1, 1), :]
            r = iota((MAIN, TOK), 0).astype(F32)
            sel.append(((even == r) | (odd == r)).astype(BF16))
            r = (iota((16, TOK), 0) % 4 + MAIN).astype(F32)
            left.append(((even == r) | (odd == r)).astype(BF16))
        sel_ref[g] = jnp.concatenate(sel, axis=0)
        left_ref[g] = jnp.concatenate(left, axis=0)
        want = (iota((TOK, PER * MAIN), 1) % MAIN).astype(F32)
        wmain_ref[g, 0], wmain_ref[g, 1] = part_weights(e, g, MAIN, want, slot_ref, weight_ref)
        want = (iota((TOK, PER * 16), 1) % 4 + MAIN).astype(F32)
        wleft_ref[g, 0], wleft_ref[g, 1] = part_weights(e, g, 16, want, slot_ref, weight_ref)
        return 0

    lax.fori_loop(0, PARTS, select, 0)
    await_bytes(vrecv.at[pl.ds(0, NEAR - 1)], v_rsem)

    def widen(i, _):
        wide_ref[pl.ds(pl.multiple_of(i * 256, 256), 256)] = vrecv[pl.ds(i * 16, 16)].astype(F32).reshape(256, 128)
        return 0

    lax.fori_loop(0, BLOCKS, widen, 0)
    for c in range(CH):
        for half in range(2):
            x_ref[c, :, 128 * half : 128 * half + 128] = wide_ref[pl.ds(8 * half + c, 256, stride=16), :]

    def conv(c, _):
        x = x_ref[c]
        lhs = x.astype(BF16)
        acc_ref[...] = x * skip_ref[e * CH + c]
        for k in range(BLOCKS):
            upper = bank_ref[c, :, PAD + 256 * k : PAD + 256 * k + 256]
            lower = bank_ref[c, :, 256 * k : 256 * k + 256]
            acc_ref[16 * k :, :] += mm(lhs[: 256 - 16 * k], jnp.concatenate([upper, lower], axis=0))
        x_ref[c] = acc_ref[...]
        return 0

    lax.fori_loop(0, CH, conv, 0)
    for c in range(CH):
        for half in range(2):
            wide_ref[pl.ds(8 * half + c, 256, stride=16), :] = x_ref[c, :, 128 * half : 128 * half + 128]

    def narrow(i, _):
        csend[pl.ds(i * 16, 16)] = wide_ref[pl.ds(pl.multiple_of(i * 256, 256), 256)].reshape(16, 16, 128).astype(BF16)
        return 0

    lax.fori_loop(0, BLOCKS, narrow, 0)

    def send_back(i, _):
        there = (z + arrival(i)) % GROUPS

        def send_plane(order, _):
            target = device(order)
            place = (target % 2 * GROUPS + there) * SEQS + target // 2
            remote(csend.at[place], crecv.at[i, e], c_ssem, c_rsem.at[i], target, there)
            return 0

        lax.fori_loop(0, HOMES - 1, send_plane, 0)

        @pl.when(there != z)
        def _():
            place = (e % 2 * GROUPS + there) * SEQS + e // 2
            remote(csend.at[place], crecv.at[i, e], c_ssem, c_rsem.at[i], e, there)

        return 0

    lax.fori_loop(0, GROUPS, send_back, 0)
    pltpu.make_async_copy(csend.at[row], crecv.at[0, e], c_rsem.at[0]).start()

    groups = [(z + GROUPS - arrival(jnp.int32(i))) % GROUPS for i in range(GROUPS)]

    def take(i, total):
        group = (z + GROUPS - arrival(i)) % GROUPS
        cols, mine = group_cols(group), group_cols(i)
        gated = branch(gate_in_ref, 0, cols, gate_kern_ref[:, cols])
        hidden = resid_ref[:, cols].astype(F32) + gated * from_message(crecv[i])
        hid_ref[:, mine] = hidden
        normed_ref[:, mine] = (hidden * gain_ref[:, cols]).astype(BF16)
        return total + jnp.sum(hidden * hidden, axis=1, keepdims=True)

    def take_two(q, total):
        await_bytes(crecv.at[2 * q], c_rsem.at[2 * q])
        total = take(2 * q, total)
        await_bytes(crecv.at[2 * q + 1], c_rsem.at[2 * q + 1])
        return take(2 * q + 1, total)

    def main_rows(q, g):
        cols = pl.ds(pl.multiple_of(QW * q, QW), QW)
        block = mm(sel_ref[g], normed_ref[:, cols]).astype(BF16).reshape(PER, MAIN, QW)
        send[pl.ds(PER * g, PER), pl.ds(pl.multiple_of(MAIN * q, MAIN), MAIN), :] = block

    def each_partner(g, action):
        for j in range(PER - 1):
            action(PER * g + j)

        @pl.when(g < PARTS - 1)
        def _():
            action(PER * g + PER - 1)

    def dispatch_early(q, total):
        total = take_two(q, total)

        def one_part(g, _):
            main_rows(q, g)
            rows = pl.ds(pl.multiple_of(MAIN * q, MAIN), MAIN)
            each_partner(
                g, lambda o: remote(send.at[o, rows], recv.at[o, rows], d_ssem, d_rsem.at[g], device(o), z)
            )
            return 0

        lax.fori_loop(0, PARTS, one_part, 0)
        return total

    total = lax.fori_loop(0, QUARTERS - 1, dispatch_early, jnp.zeros((TOK, 1), F32))
    total = take_two(QUARTERS - 1, total)
    scale = lax.rsqrt(total * (1.0 / WIDTH) + 1e-05)

    def dispatch_last(g, _):
        main_rows(QUARTERS - 1, g)
        part = iota((16 * PER, TOK), 0) % 16 // 4
        spill = jnp.zeros((16 * PER, QW), F32)
        wide = left_ref[g].astype(F32)
        for q in range(QUARTERS):
            spill += mm(jnp.where(part == q, wide, 0.0).astype(BF16), normed_ref[:, QW * q : QW * q + QW])
        send[pl.ds(PER * g, PER), MAIN * QUARTERS :, :] = spill.astype(BF16).reshape(PER, 16, QW)
        lines = []
        for per in (MAIN, 16):
            want = iota((TOK, PER * per), 1) % (MAIN if per == MAIN else 4) + (0 if per == MAIN else MAIN)
            hit = part_hits(e, g, per, want.astype(F32), slot_ref)
            lines.append(jnp.sum(jnp.where(hit[0] | hit[1], scale, 0.0), axis=0, keepdims=True))
        ssend[g] = jnp.concatenate(
            [lines[0][:, :128], lines[0][:, 128:], lines[1], jnp.zeros((5, 128), F32)], axis=0
        )
        rows = pl.ds(MAIN * (QUARTERS - 1), MAIN + 16)

        def action(o):
            remote(send.at[o, rows], recv.at[o, rows], d_ssem, d_rsem.at[g], device(o), z)
            remote(ssend.at[g], srecv.at[o], s_ssem, s_rsem.at[g], device(o), z)

        each_partner(g, action)

        @pl.when(g == PARTS - 1)
        def _():
            pltpu.make_async_copy(send.at[HOMES - 1], recv.at[HOMES - 1], d_rsem.at[g]).start()
            pltpu.make_async_copy(ssend.at[g], srecv.at[HOMES - 1], s_rsem.at[g]).start()

        return 0

    lax.fori_loop(0, PARTS, dispatch_last, 0)
    for copy in weights:
        copy.wait()
    hot = spare_ref[(e + 16) % 32]

    def expert(g, _):
        await_bytes(recv.at[pl.ds(PER * g, PER)], d_rsem.at[g])
        await_bytes(srecv.at[pl.ds(PER * g, PER)], s_rsem.at[g])
        ffn_group(g, groups, srecv, recv, wg_ref, wu_ref, wd_ref, give, hot)
        each_partner(g, lambda o: remote(give.at[o], ret.at[o], r_ssem, r_rsem.at[g], device(o, -1), z))

        @pl.when(g == PARTS - 1)
        def _():
            pltpu.make_async_copy(give.at[HOMES - 1], ret.at[HOMES - 1], r_rsem.at[g]).start()

        return 0

    lax.fori_loop(0, PARTS, expert, 0)

    def combine(g, _):
        await_bytes(ret.at[pl.ds(PER * g, PER)], r_rsem.at[g])
        left = ret[pl.ds(PER * g, PER), MAIN * QUARTERS :, :].reshape(PER * 16, QW)
        part = iota((TOK, PER * 16), 1) % 16 // 4
        for q in range(QUARTERS):
            main = ret[pl.ds(PER * g, PER), MAIN * q : MAIN * q + MAIN, :].reshape(PER * MAIN, QW)
            moe = mm(wmain_ref[g, 0], main) + mm(wmain_ref[g, 1], main)
            for w in range(2):
                moe += mm(jnp.where(part == q, wleft_ref[g, w].astype(F32), 0.0).astype(BF16), left)
            cut = slice(QW * q, QW * q + QW)
            hid_ref[:, cut] += moe
        return 0

    lax.fori_loop(0, PARTS, combine, 0)
    for i in range(GROUPS):
        out_ref[:, group_cols(groups[i])] = hid_ref[:, 256 * i : 256 * i + 256].astype(BF16)
    await_bytes(rims.at[0], t_ssem.at[0])
    await_bytes(rims.at[1], t_ssem.at[1])
    await_bytes(fsend.at[pl.ds(0, HOMES - 1)], f_ssem)
    await_bytes(csend.at[pl.ds(0, NEAR - 1)], v_ssem)
    await_bytes(csend.at[pl.ds(0, NEAR - 1)], c_ssem)
    await_bytes(srecv.at[pl.ds(0, HOMES - 1)], s_ssem)
    await_bytes(send.at[pl.ds(0, HOMES - 1)], d_ssem)
    await_bytes(send.at[pl.ds(0, HOMES - 1)], r_ssem)


def body(
    resid,
    gate_in,
    gate_short,
    value_short,
    long_filter,
    skip_gain,
    norm_gain,
    expert_ids,
    gate_wts,
    spare_pick,
    w_gate,
    w_up,
    w_down,
):
    vmem, smem, anywhere = (pl.BlockSpec(memory_space=space) for space in (pltpu.VMEM, pltpu.SMEM, pl.ANY))
    dma = pltpu.SemaphoreType.DMA
    message = pltpu.VMEM((HOMES, MSG, QW), BF16)
    pieces = pltpu.VMEM((NEAR, 16, 128), BF16)
    by_group = pltpu.VMEM((GROUPS, HOMES, 16, 128), BF16)
    taps = pltpu.VMEM((HOMES, CH, 128), F32)
    scratch = [
        by_group,
        pieces,
        taps,
        taps,
        pieces,
        by_group,
        pltpu.VMEM((2, 16, WIDTH), BF16),
        pltpu.VMEM((POS, 128), F32),
        pltpu.VMEM((CH, POS), F32),
        pltpu.VMEM((CH, 256, 256), F32),
        pltpu.VMEM((CH, 128, PAD + POS), BF16),
        pltpu.VMEM((256, 256), F32),
        pltpu.VMEM((TOK, WIDTH), F32),
        pltpu.VMEM((TOK, WIDTH), BF16),
        pltpu.VMEM((64, TOK), F32),
        pltpu.VMEM((TOK, 64), BF16),
        pltpu.VMEM((2, TOK, 64), BF16),
        pltpu.VMEM((PARTS, PER * MAIN, TOK), BF16),
        pltpu.VMEM((PARTS, PER * 16, TOK), BF16),
        pltpu.VMEM((PARTS, 2, TOK, PER * MAIN), BF16),
        pltpu.VMEM((PARTS, 2, TOK, PER * 16), BF16),
        message,
        message,
        message,
        message,
        pltpu.VMEM((PARTS, 8, 128), F32),
        pltpu.VMEM((HOMES, 8, 128), F32),
        pltpu.VMEM(w_gate.shape, BF16),
        pltpu.VMEM(w_up.shape, BF16),
        pltpu.VMEM(w_down.shape, BF16),
        pltpu.SemaphoreType.REGULAR,
        dma((3,)),
        dma((2,)),
        dma((2,)),
        dma,
        dma,
        dma,
        dma,
        dma,
        dma((GROUPS,)),
        dma,
        dma((PARTS,)),
        dma,
        dma((PARTS,)),
        dma,
        dma((PARTS,)),
    ]
    return pl.pallas_call(
        layer_kernel,
        out_shape=jax.ShapeDtypeStruct((TOK, WIDTH), BF16),
        in_specs=[smem] * 2 + [vmem] * 9 + [anywhere] * 3,
        out_specs=vmem,
        scratch_shapes=scratch,
        compiler_params=pltpu.CompilerParams(vmem_limit_bytes=VMEM_LIMIT, collective_id=0, has_side_effects=True),
        name="layer",
    )(
        spare_pick,
        skip_gain,
        resid,
        gate_in,
        gate_short,
        value_short,
        long_filter,
        norm_gain.reshape(1, WIDTH),
        expert_ids.T,
        gate_wts.T,
        spare_pick.reshape(1, HOMES),
        w_gate,
        w_up,
        w_down,
    )


def solution(mesh):
    placed = (
        P(("expert", "seq"), None),
        P(("expert", "seq"), None),
        P(),
        P(),
        P("expert", "seq"),
        P("seq"),
        P(),
        P(("expert", "seq"), None),
        P(("expert", "seq"), None),
        P(),
        P("expert", None, None),
        P("expert", None, None),
        P("expert", None, None),
    )
    return jax.shard_map(
        body, mesh=mesh, in_specs=placed, out_specs=P(("expert", "seq"), None), check_vma=False
    )
```

time: 249 us -> 195 us (0.78)
  the two profiles are of different devices: /device:TPU:53 before, /device:TPU:35 now
where the time goes in v3:
time: 195 us
  Pallas kernels  193 us (99%)
  local copies, waits for them, and re-layouts  2.3 us (1%)
    pallas_call x1, Pallas kernels, body(): pl.pallas_call(layer_kernel, out_shape=jax.ShapeDtypeStruct((TOK, WIDTH),...  193 us

profile of v3, /device:TPU:35, one launch (start us, length us, event | category | flops | bytes accessed | tf_op | source)
XLA Modules:
  0.0 194.9 jit_solution(15056985359183340106)
XLA Ops:
  0.0 192.6 %layer.1 = bf16[256,2048]{1,0:T(8,128)(2,1)} custom-call(s32[32]{0:T(128)} %spare_ref.1, f32[256]{0:T(256)} %skip_ref.1, bf16[256,2048]{1,0:T(8,128)(2,1)} %resid_ref.1, bf16[256,2048]{1,0:T(8,128)(2,1)} %gate_in_ref.1, f32[3,2048]{1,0:T(4,128)} %gate_kern_ref.1, f32[3,2048]{1,0:T(4,128)} %value_kern_ref.1, bf16[128,256]{1,0:T(8,128)(2,1)} %filt_ref.1, ...), custom_call_target="tpu_custom_call" | custom-call | tf_op jit(solution)/shard_map/layer/pallas_call | solution.py:594
  192.6 2.3 %copy.15 = bf16[256,2048]{1,0:T(8,128)(2,1)} copy(bf16[256,2048]{1,0:T(8,128)(2,1)} %layer.1) | data formatting | bytes 2097152

commit v4 on v3

--- a/solution.py
+++ b/solution.py
@@ -16,6 +16,10 @@
 SEQS = 16
 BLOCKS = 16
 CH = 8
+HALVES = 2
+SUBS = 16
+ROWS = SEQS // HALVES * BLOCKS
+PIECES = HALVES * GROUPS
 POS = SEQS * TOK
 QUARTERS = 4
 QW = WIDTH // QUARTERS
@@ -25,7 +29,7 @@
 CAP = 12
 HID = 256
 PAD = 128
-NEAR = HOMES * GROUPS
+NEAR = SUBS * GROUPS
 PARTS = 4
 PER = HOMES // PARTS
 MESH = pl.DeviceIdType.MESH
@@ -66,8 +70,8 @@
 
 def from_message(message):
     wide = message.astype(F32)
-    first = wide[:, :8].reshape(256, 128).astype(BF16)
-    second = wide[:, 8:].reshape(256, 128).astype(BF16)
+    first = wide[:, :8].reshape(128, 128).astype(BF16)
+    second = wide[:, 8:].reshape(128, 128).astype(BF16)
     ident = eye(128)
     return jnp.concatenate([nt(ident, first), nt(ident, second)], axis=0)
 
@@ -160,7 +164,7 @@
     return jnp.concatenate(cols, axis=0)
 
 
-def ffn_group(g, groups, scales, recv_ref, wg_ref, wu_ref, wd_ref, out_ref, hot):
+def ffn_group(g, rows_of, scales, recv_ref, wg_ref, wu_ref, wd_ref, out_ref, hot):
     cold = 1 - hot
     n = PER
     src = pl.ds(g * PER, n)
@@ -174,12 +178,11 @@
         xa = recv_ref[src, MAIN * q : MAIN * q + 16, lanes].reshape(rows, 256)
         xb = recv_ref[src, MAIN * q + 16 : MAIN * q + 32, lanes].reshape(rows, 256)
         left = recv_ref[src, MAIN * QUARTERS :, lanes].reshape(rows, 256)
-        cut = group_cols(groups[i])
         both = jnp.concatenate([xa, xb], axis=0)
-        gh, uh = mm(both, wg_ref[hot, cut, :]), mm(both, wu_ref[hot, cut, :])
+        gh, uh = mm(both, rows_of(wg_ref, hot, i)), mm(both, rows_of(wu_ref, hot, i))
         ga, ua, gb, ub = ga + gh[:rows], ua + uh[:rows], gb + gh[rows:], ub + uh[rows:]
         both = jnp.concatenate([xb, left], axis=0)
-        gh, uh = mm(both, wg_ref[cold, cut, :]), mm(both, wu_ref[cold, cut, :])
+        gh, uh = mm(both, rows_of(wg_ref, cold, i)), mm(both, rows_of(wu_ref, cold, i))
         gc, uc = gc + gh[:rows], uc + uh[:rows]
         gl = gl + jnp.where(part == q, gh[rows:], 0.0)
         ul = ul + jnp.where(part == q, uh[rows:], 0.0)
@@ -209,9 +212,8 @@
     for i in range(GROUPS):
         q = i // 2
         lanes = slice(256 * (i % 2), 256 * (i % 2) + 256)
-        cut = group_cols(groups[i])
-        oh = nt(hot_in, wd_ref[hot, cut, :])
-        oc = nt(cold_in, wd_ref[cold, cut, :])
+        oh = nt(hot_in, rows_of(wd_ref, hot, i))
+        oc = nt(cold_in, rows_of(wd_ref, cold, i))
         out_ref[src, MAIN * q : MAIN * q + 16, lanes] = oh[:rows].astype(BF16).reshape(n, 16, 256)
         out_ref[src, MAIN * q + 16 : MAIN * q + 32, lanes] = (oh[rows:] + oc[:rows]).astype(BF16).reshape(n, 16, 256)
         spill[i % 2] = jnp.where(part == q, oc[rows:], spill[i % 2])
@@ -221,13 +223,15 @@
 def layer_kernel(
     spare_ref, skip_ref, resid_ref, gate_in_ref, gate_kern_ref, value_kern_ref, filt_ref, gain_ref, idst_ref, wtst_ref,
     row_ref, wg_hbm, wu_hbm, wd_hbm, out_ref,
-    vsend, vrecv, fsend, frecv, csend, crecv, rims, wide_ref, hrow_ref, x_ref, bank_ref, acc_ref,
+    vsend, vrecv, fsend, frecv, csend, crecv, tail_send, tail_recv, rim_ref, wide_ref, hrow_ref, x_ref, bank_ref, acc_ref,
     hid_ref, normed_ref, slott_ref, slot_ref, weight_ref, sel_ref, left_ref, wmain_ref, wleft_ref,
     send, recv, give, ret, ssend, srecv, wg_ref, wu_ref, wd_ref,
     b_sem, w_sem, t_ssem, t_rsem, f_ssem, f_rsem, v_ssem, v_rsem, c_ssem, c_rsem, s_ssem, s_rsem, d_ssem, d_rsem, r_ssem, r_rsem,
 ):
     e, z = lax.axis_index("expert"), lax.axis_index("seq")
 
+    sub, side = e // 8 * 4 + e % 4, e // 4 % 2
+
     def device(order, sign=1):
         return ahead(e, partner(order), sign)
 
@@ -240,6 +244,9 @@
         pltpu.make_async_copy(ref, ref, sem).wait()
 
     barrier = pltpu.get_barrier_semaphore()
+    before = ((e + HOMES - 1 + (z + GROUPS - 1) // GROUPS) % HOMES, (z + GROUPS - 1) % GROUPS)
+    after = ((e + (z + 1) // GROUPS) % HOMES, (z + 1) % GROUPS)
+    pl.semaphore_signal(barrier, inc=1, device_id=before, device_id_type=MESH)
 
     def greet_line(dz, _):
         pl.semaphore_signal(barrier, inc=1, device_id=(e, (z + dz) % GROUPS), device_id_type=MESH)
@@ -258,37 +265,61 @@
     for copy in weights:
         copy.start()
     ident = eye(256)
-    fsend[...] = nt(ident, filt_ref[...]).reshape(HOMES, CH, 128)
-    pl.semaphore_wait(barrier, GROUPS - 1 + HOMES - 1)
+    flipped = nt(ident, filt_ref[...]).reshape(HALVES, SUBS, CH, 128)
+    for h in range(HALVES):
+        fsend[:, h] = flipped[h]
+    tail = jnp.concatenate(
+        [ref[TOK - 16 :, :].astype(F32)[14:16] for ref in (gate_in_ref, resid_ref)], axis=0
+    )
+    tail_send[...] = jnp.concatenate([tail[:, QW * q : QW * q + QW] for q in range(QUARTERS)], axis=0).astype(BF16)
+    pl.semaphore_wait(barrier, GROUPS - 1 + HOMES - 1 + 1)
+
+    remote(tail_send, tail_recv, t_ssem, t_rsem, *after)
 
     def greet_again(dz, _):
         pl.semaphore_signal(b_sem, inc=1, device_id=(e, (z + dz) % GROUPS), device_id_type=MESH)
         return 0
 
     lax.fori_loop(1, GROUPS, greet_again, 0)
-    pl.semaphore_wait(b_sem, GROUPS - 1)
-
-    following = ((e + (z + 1) // GROUPS) % HOMES, (z + 1) % GROUPS)
-    remote(gate_in_ref.at[pl.ds(TOK - 16, 16)], rims.at[0], t_ssem.at[0], t_rsem.at[0], *following)
-    remote(resid_ref.at[pl.ds(TOK - 16, 16)], rims.at[1], t_ssem.at[1], t_rsem.at[1], *following)
 
     def send_filter(order, _):
         target = device(order)
-        remote(fsend.at[target], frecv.at[e], f_ssem, f_rsem, target, z)
+        remote(fsend.at[target // 8 * 4 + target % 4], frecv.at[e], f_ssem, f_rsem, target, z)
         return 0
 
     lax.fori_loop(0, HOMES - 1, send_filter, 0)
-    frecv[e] = fsend[e]
+    frecv[e] = fsend[sub]
     at_start = (z == 0) & (e % 2 == 0)
 
     def branch(ref, which, cols, kernel):
-        tail = rims[which, :, cols].astype(F32)
-        tail = jnp.where(at_start, 0.0, tail)
-        return short_conv(ref[:, cols].astype(F32), tail[14:15], tail[15:16], kernel)
-
-    await_bytes(rims.at[0], t_rsem.at[0])
-    await_bytes(rims.at[1], t_rsem.at[1])
-    row = (e % 2 * GROUPS + z) * SEQS + e // 2
+        return short_conv(
+            ref[:, cols].astype(F32), rim_ref[2 * which : 2 * which + 1, cols], rim_ref[2 * which + 1 : 2 * which + 2, cols], kernel
+        )
+
+    def mate(t):
+        target = (e // 8 + t // 4) % 4 * 8 + side * 4 + (e // 2 + t // 2) % 2 * 2 + (e + t) % 2
+        return target, target // 8 * 4 + target % 4
+
+    def place_of(expert, seq):
+        return (expert % 2 * GROUPS + seq) * (SEQS // HALVES) + expert // 8 * 2 + expert // 2 % 2
+
+    await_bytes(tail_recv, t_rsem)
+    tail = tail_recv[...].astype(F32)
+    for q in range(QUARTERS):
+        rim_ref[:, QW * q : QW * q + QW] = jnp.where(at_start, 0.0, tail[4 * q : 4 * q + 4])
+    row = place_of(e, z)
+
+    def send_values(h, there):
+        def one(t, _):
+            target, share = mate(t)
+            remote(vsend.at[there, h * SUBS + share], vrecv.at[h, row], v_ssem, v_rsem.at[h], target, there)
+            return 0
+
+        lax.fori_loop(1, SUBS, one, 0)
+
+        @pl.when(there != z)
+        def _():
+            remote(vsend.at[there, h * SUBS + sub], vrecv.at[h, row], v_ssem, v_rsem.at[h], e, there)
 
     def make_values(r, _):
         there = (z + 3 * r + 4) % GROUPS
@@ -296,32 +327,37 @@
         values = branch(resid_ref, 1, cols, value_kern_ref[:, cols]).astype(BF16)
         vsend[there] = to_message(nt(ident, values))
 
-        def send_values(order, _):
-            target = device(order)
-            remote(vsend.at[there, target], vrecv.at[row], v_ssem, v_rsem, target, there)
-            return 0
-
-        lax.fori_loop(0, HOMES - 1, send_values, 0)
-
-        @pl.when(there != z)
+        @pl.when(r == 0)
         def _():
-            remote(vsend.at[there, e], vrecv.at[row], v_ssem, v_rsem, e, there)
-
+            pl.semaphore_wait(b_sem, GROUPS - 1)
+
+        send_values(0, there)
         return 0
 
     lax.fori_loop(0, GROUPS, make_values, 0)
-    vrecv[row] = vsend[z, e]
+
+    def rest_of_values(r, _):
+        send_values(1, (z + 3 * r + 4) % GROUPS)
+        return 0
+
+    lax.fori_loop(0, GROUPS, rest_of_values, 0)
+    for h in range(HALVES):
+        vrecv[h, row] = vsend[z, h * SUBS + sub]
 
     await_bytes(frecv.at[pl.ds(0, HOMES - 1)], f_rsem)
     for d in range(HOMES):
-        hrow_ref[:, 128 * d : 128 * d + 128] = frecv[d]
+        for h in range(HALVES):
+            hrow_ref[CH * h : CH * h + CH, 128 * d : 128 * d + 128] = frecv[d, h]
     bank_ref[:, :, :PAD] = jnp.zeros((CH, 128, PAD), BF16)
 
-    def bank(c, _):
-        build_bank(hrow_ref[pl.ds(c, 1), :], bank_ref.at[c])
-        return 0
-
-    lax.fori_loop(0, CH, bank, 0)
+    def make_bank(h):
+        def bank(c, _):
+            build_bank(hrow_ref[pl.ds(CH * h + c, 1), :], bank_ref.at[c])
+            return 0
+
+        lax.fori_loop(0, CH, bank, 0)
+
+    make_bank(0)
     prepare_routing(row_ref, idst_ref, wtst_ref, slott_ref, slot_ref, weight_ref)
 
     def select(g, _):
@@ -344,76 +380,73 @@
         return 0
 
     lax.fori_loop(0, PARTS, select, 0)
-    await_bytes(vrecv.at[pl.ds(0, NEAR - 1)], v_rsem)
-
-    def widen(i, _):
-        wide_ref[pl.ds(pl.multiple_of(i * 256, 256), 256)] = vrecv[pl.ds(i * 16, 16)].astype(F32).reshape(256, 128)
-        return 0
-
-    lax.fori_loop(0, BLOCKS, widen, 0)
-    for c in range(CH):
-        for half in range(2):
-            x_ref[c, :, 128 * half : 128 * half + 128] = wide_ref[pl.ds(8 * half + c, 256, stride=16), :]
-
-    def conv(c, _):
-        x = x_ref[c]
-        lhs = x.astype(BF16)
-        acc_ref[...] = x * skip_ref[e * CH + c]
-        for k in range(BLOCKS):
-            upper = bank_ref[c, :, PAD + 256 * k : PAD + 256 * k + 256]
-            lower = bank_ref[c, :, 256 * k : 256 * k + 256]
-            acc_ref[16 * k :, :] += mm(lhs[: 256 - 16 * k], jnp.concatenate([upper, lower], axis=0))
-        x_ref[c] = acc_ref[...]
-        return 0
-
-    lax.fori_loop(0, CH, conv, 0)
-    for c in range(CH):
-        for half in range(2):
-            wide_ref[pl.ds(8 * half + c, 256, stride=16), :] = x_ref[c, :, 128 * half : 128 * half + 128]
-
-    def narrow(i, _):
-        csend[pl.ds(i * 16, 16)] = wide_ref[pl.ds(pl.multiple_of(i * 256, 256), 256)].reshape(16, 16, 128).astype(BF16)
-        return 0
-
-    lax.fori_loop(0, BLOCKS, narrow, 0)
-
-    def send_back(i, _):
-        there = (z + arrival(i)) % GROUPS
-
-        def send_plane(order, _):
-            target = device(order)
-            place = (target % 2 * GROUPS + there) * SEQS + target // 2
-            remote(csend.at[place], crecv.at[i, e], c_ssem, c_rsem.at[i], target, there)
+    def convolve(h):
+        await_bytes(vrecv.at[h, pl.ds(0, NEAR - 1)], v_rsem.at[h])
+        for i in range(8):
+            wide_ref[256 * i : 256 * i + 256] = vrecv[h, 16 * i : 16 * i + 16].astype(F32).reshape(256, 128)
+        for c in range(CH):
+            for half in range(2):
+                x_ref[c, :, 128 * half : 128 * half + 128] = wide_ref[pl.ds(8 * half + c, ROWS, stride=16), :]
+
+        def conv(c, _):
+            acc_ref[...] = x_ref[c] * skip_ref[h * SUBS * CH + sub * CH + c]
+            for k in range(BLOCKS):
+                upper = bank_ref[c, :, PAD + 256 * k : PAD + 256 * k + 256]
+                lower = bank_ref[c, :, 256 * k : 256 * k + 256]
+                lhs = x_ref[c, : ROWS - 8 * k, :].astype(BF16)
+                acc_ref[8 * k :, :] += mm(lhs, jnp.concatenate([upper, lower], axis=0))
+            x_ref[c] = acc_ref[...]
             return 0
 
-        lax.fori_loop(0, HOMES - 1, send_plane, 0)
-
-        @pl.when(there != z)
-        def _():
-            place = (e % 2 * GROUPS + there) * SEQS + e // 2
-            remote(csend.at[place], crecv.at[i, e], c_ssem, c_rsem.at[i], e, there)
-
-        return 0
-
-    lax.fori_loop(0, GROUPS, send_back, 0)
-    pltpu.make_async_copy(csend.at[row], crecv.at[0, e], c_rsem.at[0]).start()
-
-    groups = [(z + GROUPS - arrival(jnp.int32(i))) % GROUPS for i in range(GROUPS)]
-
-    def take(i, total):
-        group = (z + GROUPS - arrival(i)) % GROUPS
-        cols, mine = group_cols(group), group_cols(i)
+        lax.fori_loop(0, CH, conv, 0)
+        for c in range(CH):
+            for half in range(2):
+                wide_ref[pl.ds(8 * half + c, ROWS, stride=16), :] = x_ref[c, :, 128 * half : 128 * half + 128]
+        for i in range(8):
+            csend[h, 16 * i : 16 * i + 16] = wide_ref[256 * i : 256 * i + 256].reshape(16, 16, 128).astype(BF16)
+
+        def send_back(i, _):
+            there = (z + arrival(i)) % GROUPS
+            sem = c_rsem.at[h * GROUPS + i]
+
+            def send_plane(t, _):
+                target, _ = mate(t)
+                remote(csend.at[h, place_of(target, there)], crecv.at[h, i, sub], c_ssem, sem, target, there)
+                return 0
+
+            lax.fori_loop(1, SUBS, send_plane, 0)
+
+            @pl.when(there != z)
+            def _():
+                remote(csend.at[h, place_of(e, there)], crecv.at[h, i, sub], c_ssem, sem, e, there)
+
+            return 0
+
+        lax.fori_loop(0, GROUPS, send_back, 0)
+        pltpu.make_async_copy(csend.at[h, row], crecv.at[h, 0, sub], c_rsem.at[h * GROUPS]).start()
+
+    convolve(0)
+    make_bank(1)
+
+    def piece_cols(p):
+        group = (z + GROUPS - arrival(p % GROUPS)) % GROUPS
+        return pl.ds(pl.multiple_of(group * 256 + p // GROUPS * 128, 128), 128)
+
+    def rows_of(ref, which, i):
+        return jnp.concatenate([ref[which, piece_cols(jnp.int32(p)), :] for p in (2 * i, 2 * i + 1)], axis=0)
+
+    def take(p, total):
+        h, i = p // GROUPS, p % GROUPS
+        await_bytes(crecv.at[h, i], c_rsem.at[p])
+        cols, mine = piece_cols(p), pl.ds(pl.multiple_of(128 * p, 128), 128)
         gated = branch(gate_in_ref, 0, cols, gate_kern_ref[:, cols])
-        hidden = resid_ref[:, cols].astype(F32) + gated * from_message(crecv[i])
+        hidden = resid_ref[:, cols].astype(F32) + gated * from_message(crecv[h, i])
         hid_ref[:, mine] = hidden
         normed_ref[:, mine] = (hidden * gain_ref[:, cols]).astype(BF16)
         return total + jnp.sum(hidden * hidden, axis=1, keepdims=True)
 
-    def take_two(q, total):
-        await_bytes(crecv.at[2 * q], c_rsem.at[2 * q])
-        total = take(2 * q, total)
-        await_bytes(crecv.at[2 * q + 1], c_rsem.at[2 * q + 1])
-        return take(2 * q + 1, total)
+    def take_quarter(q, total):
+        return lax.fori_loop(4 * q, 4 * q + 4, take, total)
 
     def main_rows(q, g):
         cols = pl.ds(pl.multiple_of(QW * q, QW), QW)
@@ -429,7 +462,7 @@
             action(PER * g + PER - 1)
 
     def dispatch_early(q, total):
-        total = take_two(q, total)
+        total = take_quarter(q, total)
 
         def one_part(g, _):
             main_rows(q, g)
@@ -442,8 +475,10 @@
         lax.fori_loop(0, PARTS, one_part, 0)
         return total
 
-    total = lax.fori_loop(0, QUARTERS - 1, dispatch_early, jnp.zeros((TOK, 1), F32))
-    total = take_two(QUARTERS - 1, total)
+    total = dispatch_early(jnp.int32(0), jnp.zeros((TOK, 1), F32))
+    convolve(1)
+    total = lax.fori_loop(1, QUARTERS - 1, dispatch_early, total)
+    total = take_quarter(QUARTERS - 1, total)
     scale = lax.rsqrt(total * (1.0 / WIDTH) + 1e-05)
 
     def dispatch_last(g, _):
@@ -485,7 +520,7 @@
     def expert(g, _):
         await_bytes(recv.at[pl.ds(PER * g, PER)], d_rsem.at[g])
         await_bytes(srecv.at[pl.ds(PER * g, PER)], s_rsem.at[g])
-        ffn_group(g, groups, srecv, recv, wg_ref, wu_ref, wd_ref, give, hot)
+        ffn_group(g, rows_of, srecv, recv, wg_ref, wu_ref, wd_ref, give, hot)
         each_partner(g, lambda o: remote(give.at[o], ret.at[o], r_ssem, r_rsem.at[g], device(o, -1), z))
 
         @pl.when(g == PARTS - 1)
@@ -510,13 +545,12 @@
         return 0
 
     lax.fori_loop(0, PARTS, combine, 0)
-    for i in range(GROUPS):
-        out_ref[:, group_cols(groups[i])] = hid_ref[:, 256 * i : 256 * i + 256].astype(BF16)
-    await_bytes(rims.at[0], t_ssem.at[0])
-    await_bytes(rims.at[1], t_ssem.at[1])
-    await_bytes(fsend.at[pl.ds(0, HOMES - 1)], f_ssem)
-    await_bytes(csend.at[pl.ds(0, NEAR - 1)], v_ssem)
-    await_bytes(csend.at[pl.ds(0, NEAR - 1)], c_ssem)
+    for p in range(PIECES):
+        out_ref[:, piece_cols(jnp.int32(p))] = hid_ref[:, 128 * p : 128 * p + 128].astype(BF16)
+    await_bytes(tail_send, t_ssem)
+    await_bytes(frecv.at[pl.ds(0, HOMES - 1)], f_ssem)
+    for sem in (v_ssem, c_ssem):
+        await_bytes(csend.at[:, pl.ds(0, NEAR - 1)], sem)
     await_bytes(srecv.at[pl.ds(0, HOMES - 1)], s_ssem)
     await_bytes(send.at[pl.ds(0, HOMES - 1)], d_ssem)
     await_bytes(send.at[pl.ds(0, HOMES - 1)], r_ssem)
@@ -540,22 +574,22 @@
     vmem, smem, anywhere = (pl.BlockSpec(memory_space=space) for space in (pltpu.VMEM, pltpu.SMEM, pl.ANY))
     dma = pltpu.SemaphoreType.DMA
     message = pltpu.VMEM((HOMES, MSG, QW), BF16)
-    pieces = pltpu.VMEM((NEAR, 16, 128), BF16)
-    by_group = pltpu.VMEM((GROUPS, HOMES, 16, 128), BF16)
-    taps = pltpu.VMEM((HOMES, CH, 128), F32)
+    by_row = pltpu.VMEM((HALVES, NEAR, 16, 128), BF16)
     scratch = [
-        by_group,
-        pieces,
-        taps,
-        taps,
-        pieces,
-        by_group,
-        pltpu.VMEM((2, 16, WIDTH), BF16),
-        pltpu.VMEM((POS, 128), F32),
-        pltpu.VMEM((CH, POS), F32),
-        pltpu.VMEM((CH, 256, 256), F32),
+        pltpu.VMEM((GROUPS, HOMES, 16, 128), BF16),
+        by_row,
+        pltpu.VMEM((SUBS, HALVES, CH, 128), F32),
+        pltpu.VMEM((HOMES, HALVES, CH, 128), F32),
+        by_row,
+        pltpu.VMEM((HALVES, GROUPS, SUBS, 16, 128), BF16),
+        pltpu.VMEM((16, QW), BF16),
+        pltpu.VMEM((16, QW), BF16),
+        pltpu.VMEM((4, WIDTH), F32),
+        pltpu.VMEM((ROWS * 16, 128), F32),
+        pltpu.VMEM((HALVES * CH, POS), F32),
+        pltpu.VMEM((CH, ROWS, 256), F32),
         pltpu.VMEM((CH, 128, PAD + POS), BF16),
-        pltpu.VMEM((256, 256), F32),
+        pltpu.VMEM((ROWS, 256), F32),
         pltpu.VMEM((TOK, WIDTH), F32),
         pltpu.VMEM((TOK, WIDTH), BF16),
         pltpu.VMEM((64, TOK), F32),
@@ -576,14 +610,14 @@
         pltpu.VMEM(w_down.shape, BF16),
         pltpu.SemaphoreType.REGULAR,
         dma((3,)),
-        dma((2,)),
-        dma((2,)),
-        dma,
-        dma,
-        dma,
-        dma,
-        dma,
-        dma((GROUPS,)),
+        dma,
+        dma,
+        dma,
+        dma,
+        dma,
+        dma((HALVES,)),
+        dma,
+        dma((PIECES,)),
         dma,
         dma((PARTS,)),
         dma,

time: 195 us -> 178 us (0.913)
  the two profiles are of different devices: /device:TPU:35 before, /device:TPU:1 now
where the time goes in v4:
time: 178 us; the launch traced here: 177 us
  Pallas kernels  174 us (98%)
  local copies, waits for them, and re-layouts  2.3 us (1%)
    pallas_call x1, Pallas kernels, body(): pl.pallas_call(layer_kernel, out_shape=jax.ShapeDtypeStruct((TOK, WIDTH),...  174 us

profile of v4, /device:TPU:1, one launch (start us, length us, event | category | flops | bytes accessed | tf_op | source)
XLA Modules:
  0.0 176.7 jit_solution(10342611763987660960)
XLA Ops:
  0.0 174.4 %layer.1 = bf16[256,2048]{1,0:T(8,128)(2,1)} custom-call(s32[32]{0:T(128)} %spare_ref.1, f32[256]{0:T(256)} %skip_ref.1, bf16[256,2048]{1,0:T(8,128)(2,1)} %resid_ref.1, bf16[256,2048]{1,0:T(8,128)(2,1)} %gate_in_ref.1, f32[3,2048]{1,0:T(4,128)} %gate_kern_ref.1, f32[3,2048]{1,0:T(4,128)} %value_kern_ref.1, bf16[128,256]{1,0:T(8,128)(2,1)} %filt_ref.1, ...), custom_call_target="tpu_custom_call" | custom-call | tf_op jit(solution)/shard_map/layer/pallas_call | solution.py:628
  174.4 2.3 %copy.15 = bf16[256,2048]{1,0:T(8,128)(2,1)} copy(bf16[256,2048]{1,0:T(8,128)(2,1)} %layer.1) | data formatting | bytes 2097152

commit v5 on v4

--- a/solution.py
+++ b/solution.py
@@ -77,8 +77,8 @@
 
 
 def partner(order):
-    t = (order + 1) * 11 % 32
-    return 2 * (t % 2) + t // 2 % 2, 2 * (t // 4 % 2) + t // 8 % 2, t // 16
+    t = (order + 1) * 15 % 32
+    return 2 * (t % 2) + t // 2 % 2, 2 * (t // 16) + t // 4 % 2, t // 8 % 2
 
 
 def ahead(e, offset, sign):
@@ -454,12 +454,12 @@
         send[pl.ds(PER * g, PER), pl.ds(pl.multiple_of(MAIN * q, MAIN), MAIN), :] = block
 
     def each_partner(g, action):
-        for j in range(PER - 1):
-            action(PER * g + j)
-
-        @pl.when(g < PARTS - 1)
-        def _():
-            action(PER * g + PER - 1)
+        for j in range(PER):
+            order = PER * g + (j + e) % PER
+
+            @pl.when(order != HOMES - 1)
+            def _():
+                action(order)
 
     def dispatch_early(q, total):
         total = take_quarter(q, total)
@@ -521,7 +521,9 @@
         await_bytes(recv.at[pl.ds(PER * g, PER)], d_rsem.at[g])
         await_bytes(srecv.at[pl.ds(PER * g, PER)], s_rsem.at[g])
         ffn_group(g, rows_of, srecv, recv, wg_ref, wu_ref, wd_ref, give, hot)
-        each_partner(g, lambda o: remote(give.at[o], ret.at[o], r_ssem, r_rsem.at[g], device(o, -1), z))
+        for part in range(3):
+            rows = pl.ds(48 * part, 48)
+            each_partner(g, lambda o: remote(give.at[o, rows], ret.at[o, rows], r_ssem, r_rsem.at[g], device(o, -1), z))
 
         @pl.when(g == PARTS - 1)
         def _():

time: 178 us -> 167 us (0.938)
  Pallas kernels: 174 us -> 165 us
    pallas_call x1, Pallas kernels: 174 us -> 165 us  [body(): pl.pallas_call(layer_kernel, out_shape=jax.ShapeDtypeStruct((TOK, WIDTH),...]
where the time goes in v5:
time: 167 us
  Pallas kernels  165 us (99%)
  local copies, waits for them, and re-layouts  2.3 us (1%)
    pallas_call x1, Pallas kernels, body(): pl.pallas_call(layer_kernel, out_shape=jax.ShapeDtypeStruct((TOK, WIDTH),...  165 us

profile of v5, /device:TPU:1, one launch (start us, length us, event | category | flops | bytes accessed | tf_op | source)
XLA Modules:
  0.0 167.3 jit_solution(14647283255020166837)
XLA Ops:
  0.0 164.9 %layer.1 = bf16[256,2048]{1,0:T(8,128)(2,1)} custom-call(s32[32]{0:T(128)} %spare_ref.1, f32[256]{0:T(256)} %skip_ref.1, bf16[256,2048]{1,0:T(8,128)(2,1)} %resid_ref.1, bf16[256,2048]{1,0:T(8,128)(2,1)} %gate_in_ref.1, f32[3,2048]{1,0:T(4,128)} %gate_kern_ref.1, f32[3,2048]{1,0:T(4,128)} %value_kern_ref.1, bf16[128,256]{1,0:T(8,128)(2,1)} %filt_ref.1, ...), custom_call_target="tpu_custom_call" | custom-call | tf_op jit(solution)/shard_map/layer/pallas_call | solution.py:630
  165.0 2.3 %copy.15 = bf16[256,2048]{1,0:T(8,128)(2,1)} copy(bf16[256,2048]{1,0:T(8,128)(2,1)} %layer.1) | data formatting | bytes 2097152

commit v6 on v5

--- a/solution.py
+++ b/solution.py
@@ -629,7 +629,7 @@
     ]
     return pl.pallas_call(
         layer_kernel,
-        out_shape=jax.ShapeDtypeStruct((TOK, WIDTH), BF16),
+        out_shape=pltpu.VMEM((TOK, WIDTH), BF16),
         in_specs=[smem] * 2 + [vmem] * 9 + [anywhere] * 3,
         out_specs=vmem,
         scratch_shapes=scratch,

time: 167 us -> 165 us (0.988)
  no operation moved by 1% of the time
where the time goes in v6:
time: 165 us
  Pallas kernels  164 us (99%)
    pallas_call x1, Pallas kernels, body(): pl.pallas_call(layer_kernel, out_shape=pltpu.VMEM((TOK, WIDTH), BF16), in...  164 us

profile of v6, /device:TPU:1, one launch (start us, length us, event | category | flops | bytes accessed | tf_op | source)
XLA Modules:
  0.0 165.0 jit_solution(13100748183694049326)
XLA Ops:
  0.0 164.0 %layer.1 = bf16[256,2048]{1,0:T(8,128)(2,1)S(1)} custom-call(s32[32]{0:T(128)} %spare_ref.1, f32[256]{0:T(256)} %skip_ref.1, bf16[256,2048]{1,0:T(8,128)(2,1)} %resid_ref.1, bf16[256,2048]{1,0:T(8,128)(2,1)} %gate_in_ref.1, f32[3,2048]{1,0:T(4,128)} %gate_kern_ref.1, f32[3,2048]{1,0:T(4,128)} %value_kern_ref.1, bf16[128,256]{1,0:T(8,128)(2,1)} %filt_ref.1, ...), custom_call_target="tpu_custom_call" | custom-call | tf_op jit(solution)/shard_map/layer/pallas_call | solution.py:630
  164.0 1.0 copy.15
